TPU v7x, 128 devices: a whole 4x4x4 slice. The times are simulated.
128 devices in a mesh: dp: 2 (over y_hi), row: 4 (over x), colxdept: 16 (over z, y_lo, core).
Axes of the slice: x: 4, y: 4 (y_hi: 2, y_lo: 2; y = y_hi * 2 + y_lo), z: 4, core: 2. Of those that a mesh axis runs over, the one named last changes fastest.
Arguments:
- tokens: bfloat16 [2, 512, 12288], P('dp', 'colxdept', 'row'), may hold values from -30 to 30
- w_qkv: bfloat16 [3, 12288, 6144], P(None, 'row', 'colxdept'), may hold values from -0.0546875 to 0.0546875
- w_out: bfloat16 [6144, 12288], P('colxdept', 'row'), may hold values from -0.078125 to 0.078125
- cotangent: bfloat16 [2, 512, 12288], P('dp', 'colxdept', 'row'), may hold values from -6 to 6
Outputs:
- mixed: bfloat16 [2, 512, 12288], P('dp', 'colxdept', 'row')
- grad_tokens: bfloat16 [2, 512, 12288], P('dp', 'colxdept', 'row')
- grad_qkv: bfloat16 [3, 12288, 6144], P(None, 'row', 'colxdept')
- grad_out: bfloat16 [6144, 12288], P('colxdept', 'row')
All inputs are finite; a program needn't handle non-finite values.
Results may differ from a plain program's by a relative error of at most 0.02.
The roundings to bfloat16 on the way count: a program that leaves them out, or rounds other values in their place, can miss the bound.
Values may be sent and summed in bfloat16 or wider, within the bound.
No kernel may reach another device: no remote copies, remote signals or barrier semaphores. Data moves between devices by JAX's collectives and lax.ppermute only.
A program may use at most 128 MiB of HBM per device.

v0:
```python
import jax
import jax.numpy as jnp
from jax import lax
from jax.experimental import pallas as pl
from jax.experimental.pallas import tpu as pltpu
from jax.sharding import PartitionSpec as P

DH = 128
F32 = jnp.float32
BF16 = jnp.bfloat16
NT = (((1,), (1,)), ((), ()))
TN = (((0,), (0,)), ((), ()))
ROOM = 56 * 2**20


def dot(a, b, dims=None):
    if dims is None:
        return jnp.dot(a, b, preferred_element_type=F32)
    return lax.dot_general(a, b, dims, preferred_element_type=F32)


def call(kernel, grid, in_specs, out_specs, out_shape, flops, scratch=(), aliases=None):
    def run(*args):
        many = out_shape if isinstance(out_shape, list) else [out_shape]
        moved = sum(a.size * a.dtype.itemsize for a in [*args, *many])
        return pl.pallas_call(
            kernel,
            grid=grid,
            in_specs=in_specs,
            out_specs=out_specs,
            out_shape=out_shape,
            scratch_shapes=list(scratch),
            input_output_aliases=aliases or {},
            compiler_params=pltpu.CompilerParams(vmem_limit_bytes=ROOM),
            cost_estimate=pl.CostEstimate(flops=flops, bytes_accessed=moved, transcendentals=0),
        )(*args)

    return run


def spec(block, index):
    return pl.BlockSpec(block, index)


def whole(x):
    return pl.BlockSpec(x.shape, lambda *_: (0,) * x.ndim)


SCALAR = pl.BlockSpec(memory_space=pltpu.SMEM)


def nth_part(row, j, n, part):
    return pl.ds(pl.multiple_of((row[0] + j) % n * part, part), part)


def project(row, mine, sib, w, n_row):
    n, depth, width = w.shape
    half = mine.shape[0]
    part = 2 * half // n_row

    def kernel(row, mine, sib, w, *rest):
        outs, held = rest[:-1], rest[-1]

        @pl.when(pl.program_id(0) == 0)
        def _():
            held[:half] = mine[...]
            held[half:] = sib[...]

        for j, out in enumerate(outs):
            out[...] = dot(held[nth_part(row, j, n_row, part)], w[...])

    return call(
        kernel,
        (n,),
        [SCALAR, whole(mine), whole(sib), spec((None, depth, width), lambda a: (a, 0, 0))],
        [spec((part, width), lambda a: (0, a))] * n_row,
        [jax.ShapeDtypeStruct((part, n * width), F32)] * n_row,
        4 * half * n * depth * width,
        [pltpu.VMEM((2 * half, depth), BF16)],
    )(row, mine, sib, w)


def back_half(x, w):
    width, depth = w.shape
    half = x.shape[0]
    step = min(1024, depth)

    def kernel(x, w, out):
        @pl.when(pl.program_id(0) == 0)
        def _():
            out[...] = jnp.zeros_like(out)

        out[...] += dot(x[...], w[...], NT)

    return call(
        kernel,
        (depth // step,),
        [spec((half, step), lambda k: (0, k)), spec((width, step), lambda k: (0, k))],
        spec((half, width), lambda k: (0, 0)),
        jax.ShapeDtypeStruct((half, width), F32),
        2 * half * depth * width,
    )(x, w)


def back_context(row, mine, sib, w, n_row):
    width, depth = w.shape
    half = sib.shape[0]
    part = 2 * half // n_row
    step = min(1024, depth)

    def kernel(row, mine, sib, w, *rest):
        outs, total = rest[:-1], rest[-1]

        @pl.when(pl.program_id(0) == 0)
        def _():
            total[:half] = mine[...]
            total[half:] = jnp.zeros_like(mine)

        total[half:] += dot(sib[...], w[...], NT)

        @pl.when(pl.program_id(0) == pl.num_programs(0) - 1)
        def _():
            for j, out in enumerate(outs):
                out[...] = total[nth_part(row, j, n_row, part)]

    return call(
        kernel,
        (depth // step,),
        [
            SCALAR,
            whole(mine),
            spec((half, step), lambda k: (0, k)),
            spec((width, step), lambda k: (0, k)),
        ],
        [spec((part, width), lambda k: (0, 0))] * n_row,
        [jax.ShapeDtypeStruct((part, width), F32)] * n_row,
        2 * half * depth * width,
        [pltpu.VMEM((2 * half, width), F32)],
    )(row, mine, sib, w)


def attention(row, rows, cols, pieces, back_pieces):
    n = len(pieces)
    part, width = back_pieces[0].shape
    seq = n * part
    half, heads = seq // 2, width // DH
    scale = 1.0 / DH**0.5

    def kernel(row, rows, cols, *rest):
        parts, (out, out_sib, out_part, held) = rest[: 2 * n], rest[2 * n :]

        @pl.when(pl.program_id(0) == 0)
        def _():
            for j in range(n):
                held[nth_part(row, j, n, part), : 3 * width] = parts[j][...]
                held[nth_part(row, j, n, part), 3 * width :] = parts[n + j][...]

        h = pl.program_id(0)
        q, k, v, g = [held[:, pl.ds(pl.multiple_of((a * heads + h) * DH, DH), DH)] for a in range(4)]
        scores = dot(q, k, NT) * scale
        scores = jnp.where(rows[...] >= cols[...], scores, -1e30)
        expo = jnp.exp(scores - jnp.max(scores, axis=-1, keepdims=True))
        probs = expo / jnp.sum(expo, axis=-1, keepdims=True)
        probs_b = probs.astype(BF16)
        out[0] = dot(probs_b, v).astype(BF16)
        out[3] = dot(probs_b, g, TN).astype(BF16)
        grad_probs = dot(g, v, NT)
        delta = jnp.sum(grad_probs * probs, axis=-1, keepdims=True)
        grad_scores = (probs * (grad_probs - delta) * scale).astype(BF16)
        out[1] = dot(grad_scores, k).astype(BF16)
        out[2] = dot(grad_scores, q, TN).astype(BF16)
        out_sib[...] = out[:, half:]
        out_part[...] = out[:, nth_part(row, 0, n, part)]

    return call(
        kernel,
        (heads,),
        [SCALAR, whole(rows), whole(cols)] + [whole(x) for x in (*pieces, *back_pieces)],
        [spec((4, r, DH), lambda h: (0, 0, h)) for r in (seq, half, part)],
        [jax.ShapeDtypeStruct((4, r, width), BF16) for r in (seq, half, part)],
        14 * heads * seq * seq * DH,
        [pltpu.VMEM((seq, 4 * width), BF16)],
    )(row, rows, cols, *pieces, *back_pieces)


def mix(chips, done, done_sib, w, w_sib):
    width, depth = w.shape
    half = done_sib.shape[1]
    step = min(1024, depth)

    def kernel(d, ds, w, ws, out):
        out[...] = (dot(d[...], w[...]) + dot(ds[...], ws[...])).astype(BF16).reshape(out.shape)

    d_spec = spec((None, half, width), lambda m: (0, 0, 0))
    w_spec = spec((width, step), lambda m: (0, m))
    return call(
        kernel,
        (depth // step,),
        [d_spec, d_spec, w_spec, w_spec],
        spec((chips, None, half // chips, step), lambda m: (0, 0, 0, m)),
        jax.ShapeDtypeStruct((chips, 2, half // chips, depth), BF16),
        4 * half * depth * width,
    )(done, done_sib, w, w_sib)


def back_tokens(first, done, done_sib, w, w_sib):
    n, depth, width = w.shape
    chips, half = first.shape[0], done_sib.shape[1]
    step = min(512, depth)

    def side(x, start):
        return [x[a] for a in range(start, n + start)]

    def kernel(_, d, ds, w, ws, out):
        grads = jnp.concatenate(side(d, 1) + side(ds, 1), axis=1)
        weights = jnp.concatenate(side(w, 0) + side(ws, 0), axis=1)
        out[...] = dot(grads, weights, NT).astype(BF16).reshape(out.shape)

    d_spec = spec((n + 1, half, width), lambda m: (0, 0, 0))
    w_spec = spec((n, step, width), lambda m: (0, m, 0))
    return call(
        kernel,
        (depth // step,),
        [pl.BlockSpec(memory_space=pl.ANY), d_spec, d_spec, w_spec, w_spec],
        spec((chips, None, half // chips, step), lambda m: (0, 1, 0, m)),
        jax.ShapeDtypeStruct(first.shape, BF16),
        4 * half * n * depth * width,
        aliases={0: 0},
    )(first, done, done_sib, w, w_sib)


def weight_own(tok_mine, tok_sib, cot_mine, cot_sib, done):
    n, seq, width = done.shape[0] - 1, *done.shape[1:]
    half, depth = tok_mine.shape
    step = min(512, depth)

    def kernel(t0, t1, c0, c1, d, out_qkv, out_out, held):
        @pl.when(pl.program_id(0) == 0)
        def _():
            held[...] = d[0].T

        x = jnp.concatenate([t0[...], t1[...]], axis=0)
        for a in range(n):
            out_qkv[a] = dot(x, d[a + 1], TN)
        out_out[...] = dot(held[...], jnp.concatenate([c0[...], c1[...]], axis=0))

    x_spec = spec((half, step), lambda m: (0, m))
    return call(
        kernel,
        (depth // step,),
        [x_spec] * 4 + [whole(done)],
        [spec((n, step, width), lambda m: (0, m, 0)), spec((width, step), lambda m: (0, m))],
        [jax.ShapeDtypeStruct((n, depth, width), F32), jax.ShapeDtypeStruct((width, depth), F32)],
        2 * seq * (n + 1) * depth * width,
        [pltpu.VMEM((width, seq), BF16)],
    )(tok_mine, tok_sib, cot_mine, cot_sib, done)


def weight_both(row, own_qkv, own_out, mine, sib, pieces):
    n, depth, width = own_qkv.shape
    half = mine.shape[0]
    count, part = len(pieces), pieces[0].shape[1]
    seq = count * part
    step = min(512, depth)
    steps = depth // step

    def kernel(row, q, o, t0, t1, c0, c1, *rest):
        parts, (out_qkv, out_out, held, turned) = rest[:count], rest[count:]

        @pl.when(pl.program_id(0) == 0)
        def _():
            for j in range(count):
                rows = nth_part(row, j, count, part)
                held[:, rows] = parts[j][1:]
                turned[:, rows] = parts[j][0].T

        x = jnp.concatenate([t0[...], t1[...]], axis=0)
        for a in range(n):
            out_qkv[a] = (q[a] + dot(x, held[a], TN)).astype(BF16)
        y = jnp.concatenate([c0[...], c1[...]], axis=0)
        out_out[...] = (o[...] + dot(turned[...], y)).astype(BF16)

    t_spec = spec((half, step), lambda m: (0, m))
    c_spec = spec((half, step), lambda m: (0, steps + m))
    q_spec = spec((n, step, width), lambda m: (0, m, 0))
    o_spec = spec((width, step), lambda m: (0, m))
    return call(
        kernel,
        (steps,),
        [SCALAR, q_spec, o_spec, t_spec, t_spec, c_spec, c_spec] + [whole(x) for x in pieces],
        [q_spec, o_spec],
        [jax.ShapeDtypeStruct((n, depth, width), BF16), jax.ShapeDtypeStruct((width, depth), BF16)],
        2 * seq * (n + 1) * depth * width,
        [pltpu.VMEM((n, seq, width), BF16), pltpu.VMEM((width, seq), BF16)],
    )(row, own_qkv, own_out, mine, sib, mine, sib, *pieces)


def after(x, *others):
    return lax.optimization_barrier((x, *others))[0]


def body(tokens, w_qkv, w_out, cotangent):
    n_row = lax.axis_size("row")
    n_col = lax.axis_size("colxdept")
    n_dp = lax.axis_size("dp")
    chips = n_col // 2
    tile = tokens.shape[1]
    seq = tile * n_col
    half, local = seq // 2, seq // n_row
    core = lax.axis_index("colxdept") % 2
    row = lax.axis_index("row").astype(jnp.int32)
    at = row[None]
    same_core = [list(range(c, n_col, 2)) for c in range(2)]

    def swap_cores(x):
        return lax.ppermute(x, "colxdept", [(i, i ^ 1) for i in range(n_col)])

    def swap_dp(x):
        return lax.ppermute(x, "dp", [(i, (i + 1) % n_dp) for i in range(n_dp)])

    def along_row(x, step):
        return lax.ppermute(x, "row", [(i, (i + step) % n_row) for i in range(n_row)])

    def among_chips(x):
        return lax.all_to_all(x, "colxdept", 0, 0, axis_index_groups=same_core)

    def gather_core(x, *others):
        copies = jnp.broadcast_to(x[None], (chips, *x.shape))
        return among_chips(after(copies, *others) if others else copies).reshape(half, -1)

    def gather_row(x):
        return [x] + [along_row(x, -j) for j in range(1, n_row)]

    def to_row(parts):
        return [parts[0]] + [along_row(parts[j], j) for j in range(1, n_row)]

    def total(parts):
        return sum(parts[1:], parts[0]).astype(BF16)

    index = jnp.arange(seq, dtype=jnp.int32)
    owner = (index // half + core) % 2
    position = ((index % half) // tile * 2 + owner) * tile + index % tile
    rows, cols = position[:, None], position[None, :]

    w_out_sib = swap_cores(w_out)
    w_qkv_sib = swap_cores(w_qkv)
    tok_mine, w_out_sib, w_qkv_sib = lax.optimization_barrier((gather_core(tokens[0]), w_out_sib, w_qkv_sib))
    tok_sib = swap_cores(tok_mine)
    other = swap_dp(after(jnp.concatenate([tokens[0], cotangent[0]], axis=1), tok_mine))
    qkv_parts = project(at, tok_mine, tok_sib, w_qkv, n_row)
    cot_mine = gather_core(cotangent[0], other, *qkv_parts)
    other_mine = gather_core(other, cot_mine)
    qkv_sum = total(to_row(qkv_parts))
    pieces = gather_row(qkv_sum)
    cot_mine = after(cot_mine, qkv_sum)
    cot_sib = after(swap_cores(cot_mine), pieces[1], pieces[3])
    back_parts = back_context(at, back_half(cot_mine, w_out), cot_sib, w_out, n_row)
    back_pieces = gather_row(total(to_row(back_parts)))
    back_pieces[0] = after(back_pieces[0], other_mine)

    done, second, quarter = attention(at, rows, cols, pieces, back_pieces)
    quarter = swap_dp(quarter)
    done_sib = swap_cores(second)
    first = mix(chips, done, done_sib, w_out, w_out_sib)
    both = back_tokens(first, done, done_sib, w_qkv, w_qkv_sib)
    both, quarter, other_mine = lax.optimization_barrier((both, quarter, other_mine))
    done2 = gather_row(quarter)
    other_sib = swap_cores(other_mine)
    shares = among_chips(both)
    own_qkv, own_out = weight_own(tok_mine, tok_sib, cot_mine, cot_sib, after(done, both))
    grad_qkv, grad_out = weight_both(at, own_qkv, own_out, other_mine, other_sib, done2)
    shares = after(shares, grad_out, grad_qkv)
    results = jnp.sum(shares.astype(F32), axis=0).astype(BF16)
    return (results[:1], results[1:], grad_qkv, grad_out)


def solution(mesh):
    return jax.shard_map(
        body,
        mesh=mesh,
        in_specs=(
            P("dp", "colxdept", "row"),
            P(None, "row", "colxdept"),
            P("colxdept", "row"),
            P("dp", "colxdept", "row"),
        ),
        out_specs=(
            P("dp", "colxdept", "row"),
            P("dp", "colxdept", "row"),
            P(None, "row", "colxdept"),
            P("colxdept", "row"),
        ),
        check_vma=False,
    )
```

profile of v0, /device:TPU:1, one launch (start us, length us, event | category | flops | bytes accessed | tf_op | source)
XLA Modules:
  0.0 195.8 jit_solution(17520870934709329796)
XLA Ops:
  0.7 1.5 collective-permute-start.1
  2.2 1.1 broadcast_in_dim.27
  3.4 26.5 %all_to_all.20 = bf16[8,32,3072]{2,1,0:T(8,128)(2,1)S(1)} all-to-all(bf16[8,32,3072]{2,1,0:T(8,128)(2,1)S(1)} %broadcast_in_dim.27), channel_id=1, replica_groups={{0,2,4,6,8,10,12,14},{1,3,5,7,9,11,13,15},{16,18,20,22,24,26,28,30},{17..., dimensions={0} | all-to-all | bytes 3145728 | tf_op jit(solution)/shard_map/all_to_all | solution.py:325
  29.8 1.9 collective-permute-start.2
  31.8 2.7 %collective-permute-start.9 = (bf16[32,6144]{1,0:T(8,128)(2,1)S(1)}, bf16[32,6144]{1,0:T(8,128)(2,1)S(1)}, u32[]{:S(2)}, u32[]{:S(2)}) collective-permute-start(bf16[32,6144]{1,0:T(8,128)(2,1)S(1)} %pad_maximum_fusion), channel_id=1, source_target_pairs={{0,64},{64,0},{1,65},{65,1},{2,66},{66,2},{3,67},{67,3},{4,68},{68... | collective-permute-start | bytes 1179656 | tf_op jit(solution)/shard_map/ppermute | solution.py:319
  34.9 9.1 %shard_map.75 = (f32[128,1152]{1,0:T(8,128)}, f32[128,1152]{1,0:T(8,128)}, f32[128,1152]{1,0:T(8,128)}, f32[128,1152]{1,0:T(8,128)}) custom-call(s32[1]{0:T(128)} %bitcast.row, bf16[256,3072]{1,0:T(8,128)(2,1)} %bitcast.13, bf16[256,3072]{1,0:T(8,128)(2,1)} %collective-permute-done.2.sib.t1, bf16[3,3072,384]{2,1,0:T(8,128)(2,1)} %w.9), custom_call_target="tpu_custom_call" | custom-call | flops 3623878656 | bytes 12582916 | tf_op jit(solution)/shard_map/pallas_call | solution.py:26
  44.1 1.3 broadcast_in_dim.29
  45.4 3.6 %all-to-all-start.1 = ((bf16[8,32,3072]{2,1,0:T(8,128)(2,1)}), bf16[8,32,3072]{2,1,0:T(8,128)(2,1)S(1)}, u32[]{:S(2)}, u32[]{:S(2)}) async-start(bf16[8,32,3072]{2,1,0:T(8,128)(2,1)} %broadcast_in_dim.29), calls=%async_computation.1 | async-start | bytes 3145728 | tf_op jit(solution)/shard_map/all_to_all | solution.py:325
  49.0 1.3 collective-permute-start.3
  50.3 2.5 %collective-permute-start.4 = (f32[128,1152]{1,0:T(8,128)}, f32[128,1152]{1,0:T(8,128)}, u32[]{:S(2)}, u32[]{:S(2)}) collective-permute-start(f32[128,1152]{1,0:T(8,128)} %get-tuple-element.36), channel_id=1, source_target_pairs={{0,32},{16,48},{32,0},{48,16},{1,33},{17,49},{33,1},{49,17},{2,34}... | collective-permute-start | bytes 1769480 | tf_op jit(solution)/shard_map/ppermute | solution.py:322
  52.7 1.2 collective-permute-start.5
  53.9 15.8 %all-to-all-done.1 = bf16[8,32,3072]{2,1,0:T(8,128)(2,1)S(1)} async-done(((bf16[8,32,3072]{2,1,0:T(8,128)(2,1)}), bf16[8,32,3072]{2,1,0:T(8,128)(2,1)S(1)}, u32[]{:S(2)}, u32[]{:S(2)}) %all-to-all-start.1) | async-done | bytes 1572896 | tf_op jit(solution)/shard_map/all_to_all | solution.py:325
  69.7 2.2 %broadcast_in_dim.30 = bf16[8,32,6144]{2,1,0:T(8,128)(2,1)} broadcast(bf16[32,6144]{1,0:T(8,128)(2,1)S(1)} %collective-permute-done.9), dimensions={1,2} | broadcast | bytes 3538944 | tf_op jit(solution)/shard_map/broadcast_in_dim | solution.py:328
  71.8 3.7 %all-to-all-start.2 = ((bf16[8,32,6144]{2,1,0:T(8,128)(2,1)}), bf16[8,32,6144]{2,1,0:T(8,128)(2,1)S(1)}, u32[]{:S(2)}, u32[]{:S(2)}) async-start(bf16[8,32,6144]{2,1,0:T(8,128)(2,1)} %broadcast_in_dim.30), calls=%async_computation.2 | async-start | bytes 6291456 | tf_op jit(solution)/shard_map/all_to_all | solution.py:325
  75.5 2.8 %collective-permute-done.4 = f32[128,1152]{1,0:T(8,128)} collective-permute-done((f32[128,1152]{1,0:T(8,128)}, f32[128,1152]{1,0:T(8,128)}, u32[]{:S(2)}, u32[]{:S(2)}) %collective-permute-start.4) | collective-permute-done | bytes 589856 | tf_op jit(solution)/shard_map/ppermute | solution.py:322
  78.3 1.7 add_convert_fusion.rest_0_
  80.0 1.8 collective-permute-start.10
  81.8 1.1 collective-permute-start.8
  82.9 1.6 collective-permute-start.6
  84.5 4.3 %shard_map.76.mine = f32[256,384]{1,0:T(8,128)} custom-call(bf16[256,3072]{1,0:T(8,128)(2,1)} %bitcast.10, bf16[384,3072]{1,0:T(8,128)(2,1)} %w.8), custom_call_target="tpu_custom_call" | custom-call | flops 603979776 | bytes 4325376 | tf_op jit(solution)/shard_map/pallas_call | solution.py:26
  88.8 2.8 %collective-permute-done.8.rest_3_ = bf16[128,1152]{1,0:T(8,128)(2,1)S(1)} collective-permute-done((bf16[128,1152]{1,0:T(8,128)(2,1)S(1)}, bf16[128,1152]{1,0:T(8,128)(2,1)S(1)}, u32[]{:S(2)}, u32[]{:S(2)}) %collective-permute-start.8) | collective-permute-done | bytes 294944 | tf_op jit(solution)/shard_map/ppermute | solution.py:322
  91.6 1.1 copy-done.4
  92.7 4.6 %shard_map.77 = (f32[128,384]{1,0:T(8,128)}, f32[128,384]{1,0:T(8,128)}, f32[128,384]{1,0:T(8,128)}, f32[128,384]{1,0:T(8,128)}) custom-call(s32[1]{0:T(128)} %bitcast.row, f32[256,384]{1,0:T(8,128)} %shard_map.76.mine, bf16[256,3072]{1,0:T(8,128)(2,1)} %copy-done.4, bf16[384,3072]{1,0:T(8,128)(2,1)} %w.8), custom_call_target="tpu_custom_call" | custom-call | flops 603979776 | bytes 5111812 | tf_op jit(solution)/shard_map/pallas_call | solution.py:26
  98.0 3.0 %collective-permute-start.12 = (f32[128,384]{1,0:T(8,128)}, f32[128,384]{1,0:T(8,128)}, u32[]{:S(2)}, u32[]{:S(2)}) collective-permute-start(f32[128,384]{1,0:T(8,128)} %get-tuple-element.44), channel_id=1, source_target_pairs={{0,32},{16,48},{32,0},{48,16},{1,33},{17,49},{33,1},{49,17},{2,34}... | collective-permute-start | bytes 589832 | tf_op jit(solution)/shard_map/ppermute | solution.py:322
  101.1 0.9 fusion.4.rows
  102.0 1.3 collective-permute-start.7
  103.4 1.1 collective-permute-done.11
  104.5 4.7 %collective-permute-done.12 = f32[128,384]{1,0:T(8,128)} collective-permute-done((f32[128,384]{1,0:T(8,128)}, f32[128,384]{1,0:T(8,128)}, u32[]{:S(2)}, u32[]{:S(2)}) %collective-permute-start.12) | collective-permute-done | bytes 196640 | tf_op jit(solution)/shard_map/ppermute | solution.py:322
  109.2 1.1 collective-permute-done.13
  110.4 1.3 add_convert_fusion.1.rest_4_
  111.6 3.1 %collective-permute-start.16 = (bf16[128,384]{1,0:T(8,128)(2,1)S(1)}, bf16[128,384]{1,0:T(8,128)(2,1)}, u32[]{:S(2)}, u32[]{:S(2)}) collective-permute-start(bf16[128,384]{1,0:T(8,128)(2,1)S(1)} %add_convert_fusion.1.rest_4_), channel_id=1, source_target_pairs={{0,16},{16,32},{32,48},{48,0},{1,17},{17,33},{33,49},{49,1},{2,18}... | collective-permute-start | bytes 294920 | tf_op jit(solution)/shard_map/ppermute | solution.py:322
  114.8 2.0 %collective-permute-start.15 = (bf16[128,384]{1,0:T(8,128)(2,1)S(1)}, bf16[128,384]{1,0:T(8,128)(2,1)}, u32[]{:S(2)}, u32[]{:S(2)}) collective-permute-start(bf16[128,384]{1,0:T(8,128)(2,1)S(1)} %add_convert_fusion.1.rest_4_), channel_id=1, source_target_pairs={{0,32},{16,48},{32,0},{48,16},{1,33},{17,49},{33,1},{49,17},{2,34}... | collective-permute-start | bytes 294920 | tf_op jit(solution)/shard_map/ppermute | solution.py:322
  118.0 2.7 %collective-permute-done.15.rest_6_ = bf16[128,384]{1,0:T(8,128)(2,1)} collective-permute-done((bf16[128,384]{1,0:T(8,128)(2,1)S(1)}, bf16[128,384]{1,0:T(8,128)(2,1)}, u32[]{:S(2)}, u32[]{:S(2)}) %collective-permute-start.15) | collective-permute-done | bytes 98336 | tf_op jit(solution)/shard_map/ppermute | solution.py:322
  120.7 0.9 collective-permute-done.14.rest_5_
  121.6 7.6 %shard_map.78 = (bf16[4,512,384]{2,1,0:T(8,128)(2,1)}, bf16[4,256,384]{2,1,0:T(8,128)(2,1)}, bf16[4,128,384]{2,1,0:T(8,128)(2,1)}) custom-call(s32[1]{0:T(128)} %bitcast.row, s32[512,1]{1,0:T(8,128)} %fusion.4.rows, s32[1,512]{1,0:T(1,128)} %fusion.18.cols, bf16[128,1152]{1,0:T(8,128)(2,1)} %copy-done.11, bf16[128,1152]{1,0:T(8,128)(2,1)} %copy-done.14, ...), custom_call_target="tpu_custom_call" | custom-call | flops 1409286144 | bytes 4329476 | tf_op jit(solution)/shard_map/pallas_call | solution.py:26
  129.2 1.6 collective-permute-start.17
  130.8 2.6 %collective-permute-start.18 = (bf16[4,128,384]{2,1,0:T(8,128)(2,1)}, bf16[4,128,384]{2,1,0:T(8,128)(2,1)S(1)}, u32[]{:S(2)}, u32[]{:S(2)}) collective-permute-start(bf16[4,128,384]{2,1,0:T(8,128)(2,1)} %get-tuple-element.52), channel_id=1, source_target_pairs={{0,64},{64,0},{1,65},{65,1},{2,66},{66,2},{3,67},{67,3},{4,68},{68... | collective-permute-start | bytes 1179656 | tf_op jit(solution)/shard_map/ppermute | solution.py:319
  133.4 0.9 copy-done.2
  134.4 5.3 %shard_map.79._ = bf16[8,2,32,3072]{3,2,1,0:T(8,128)(2,1)} custom-call(bf16[4,512,384]{2,1,0:T(8,128)(2,1)} %get-tuple-element.54.d, bf16[4,256,384]{2,1,0:T(8,128)(2,1)} %copy-done.2, bf16[384,3072]{1,0:T(8,128)(2,1)} %w.8, bf16[384,3072]{1,0:T(8,128)(2,1)} %collective-permute-done.ws), custom_call_target="tpu_custom_call" | custom-call | flops 1207959552 | bytes 10223616 | tf_op jit(solution)/shard_map/pallas_call | solution.py:26
  139.6 10.0 %shard_map.80 = bf16[8,2,32,3072]{3,2,1,0:T(8,128)(2,1)} custom-call(bf16[8,2,32,3072]{3,2,1,0:T(8,128)(2,1)} %shard_map.79._, bf16[4,512,384]{2,1,0:T(8,128)(2,1)} %get-tuple-element.54.d, bf16[4,256,384]{2,1,0:T(8,128)(2,1)} %copy-done.2, bf16[3,3072,384]{2,1,0:T(8,128)(2,1)} %w.9, ...), custom_call_target="tpu_custom_call", output_to_operand_aliasing={{}: (0, {})} | custom-call | flops 3623878656 | bytes 22806528 | tf_op jit(solution)/shard_map/pallas_call | solution.py:26
  150.0 4.5 %all-to-all-start.3 = ((bf16[8,2,32,3072]{3,2,1,0:T(8,128)(2,1)}), bf16[8,2,32,3072]{3,2,1,0:T(8,128)(2,1)}, u32[]{:S(2)}, u32[]{:S(2)}) async-start(bf16[8,2,32,3072]{3,2,1,0:T(8,128)(2,1)} %shard_map.80), calls=%async_computation.3 | async-start | bytes 6291456 | tf_op jit(solution)/shard_map/all_to_all | solution.py:325
  155.1 2.6 %collective-permute-start.21 = (bf16[4,128,384]{2,1,0:T(8,128)(2,1)S(1)}, bf16[4,128,384]{2,1,0:T(8,128)(2,1)S(1)}, u32[]{:S(2)}, u32[]{:S(2)}) collective-permute-start(bf16[4,128,384]{2,1,0:T(8,128)(2,1)S(1)} %collective-permute-done.18.rest_0_), channel_id=1, source_target_pairs={{0,32},{16,48},{32,0},{48,16},{1,33},{17,49},{33,1},{49,17},{2,34}... | collective-permute-start | bytes 1179656 | tf_op jit(solution)/shard_map/ppermute | solution.py:322
  158.0 13.1 %shard_map.81 = (f32[3,3072,384]{2,1,0:T(8,128)}, f32[384,3072]{1,0:T(8,128)}) custom-call(bf16[256,3072]{1,0:T(8,128)(2,1)} %bitcast.14, bf16[256,3072]{1,0:T(8,128)(2,1)} %collective-permute-done.2.sib.t1, bf16[256,3072]{1,0:T(8,128)(2,1)} %bitcast.11, bf16[256,3072]{1,0:T(8,128)(2,1)} %copy-done.4, bf16[4,512,384]{2,1,0:T(8,128)(2,1)} %get-tuple-element.54.d), custom_call_target="tpu_custom_call" | custom-call | flops 4831838208 | bytes 26738688 | tf_op jit(solution)/shard_map/pallas_call | solution.py:26
  171.0 4.1 %collective-permute-done.21.rest_2_ = bf16[4,128,384]{2,1,0:T(8,128)(2,1)S(1)} collective-permute-done((bf16[4,128,384]{2,1,0:T(8,128)(2,1)S(1)}, bf16[4,128,384]{2,1,0:T(8,128)(2,1)S(1)}, u32[]{:S(2)}, u32[]{:S(2)}) %collective-permute-start.21) | collective-permute-done | bytes 393248 | tf_op jit(solution)/shard_map/ppermute | solution.py:322
  176.0 15.8 %shard_map.82 = (bf16[3,3072,384]{2,1,0:T(8,128)(2,1)}, bf16[384,3072]{1,0:T(8,128)(2,1)}) custom-call(s32[1]{0:T(128)} %bitcast.row, f32[3,3072,384]{2,1,0:T(8,128)} %get-tuple-element.55.q, f32[384,3072]{1,0:T(8,128)} %get-tuple-element.56.o, bf16[256,6144]{1,0:T(8,128)(2,1)} %bitcast.7, bf16[256,6144]{1,0:T(8,128)(2,1)} %collective-permute-done.19.t1.c1, ...), custom_call_target="tpu_custom_call" | custom-call | flops 4831838208 | bytes 42467332 | tf_op jit(solution)/shard_map/pallas_call | solution.py:26
  191.8 0.8 all-to-all-done.3
  192.6 2.5 %reduce_sum.12 = bf16[2,32,3072]{2,1,0:T(8,128)(2,1)S(1)} reduce(bf16[8,2,32,3072]{3,2,1,0:T(8,128)(2,1)} %all-to-all-done.3, bf16[]{:T(256)} %constant.91.clone.1), dimensions={0}, to_apply=%region_0.1 | reduce | flops 1376256 | bytes 3538946 | tf_op jit(solution)/shard_map/reduce_sum | solution.py:373
  195.0 0.8 fusion.21
  (53 shorter events, 4.8 us)
Async XLA Ops:
  0.6 31.1 %copy-start.5 = (bf16[1,32,3072]{2,1,0:T(8,128)(2,1)S(1)}, bf16[1,32,3072]{2,1,0:T(8,128)(2,1)}, u32[]{:S(2)}) copy-start(bf16[1,32,3072]{2,1,0:T(8,128)(2,1)} %param.4) | copy-start | bytes 589828
  0.6 31.1 %copy-start.6 = (bf16[1,32,3072]{2,1,0:T(8,128)(2,1)S(1)}, bf16[1,32,3072]{2,1,0:T(8,128)(2,1)}, u32[]{:S(2)}) copy-start(bf16[1,32,3072]{2,1,0:T(8,128)(2,1)} %param.7) | copy-start | bytes 589828
  0.7 29.2 %collective-permute-start.1 = (bf16[3,3072,384]{2,1,0:T(8,128)(2,1)}, bf16[3,3072,384]{2,1,0:T(8,128)(2,1)}, u32[]{:S(2)}, u32[]{:S(2)}) collective-permute-start(bf16[3,3072,384]{2,1,0:T(8,128)(2,1)} %w.9), channel_id=1, source_target_pairs={{0,1},{1,0},{2,3},{3,2},{4,5},{5,4},{6,7},{7,6},{8,9},{9,8},{10,11... | collective-permute-start | bytes 21233672 | tf_op jit(solution)/shard_map/ppermute | solution.py:316
  2.2 27.7 %collective-permute-start = (bf16[384,3072]{1,0:T(8,128)(2,1)}, bf16[384,3072]{1,0:T(8,128)(2,1)}, u32[]{:S(2)}, u32[]{:S(2)}) collective-permute-start(bf16[384,3072]{1,0:T(8,128)(2,1)} %w.8), channel_id=1, source_target_pairs={{0,1},{1,0},{2,3},{3,2},{4,5},{5,4},{6,7},{7,6},{8,9},{9,8},{10,11... | collective-permute-start | bytes 7077896 | tf_op jit(solution)/shard_map/ppermute | solution.py:316
  29.8 5.1 %copy-start.3 = (bf16[8,32,3072]{2,1,0:T(8,128)(2,1)}, bf16[8,32,3072]{2,1,0:T(8,128)(2,1)S(1)}, u32[]{:S(2)}) copy-start(bf16[8,32,3072]{2,1,0:T(8,128)(2,1)S(1)} %all_to_all.20) | copy-start | bytes 4718596
  29.8 5.1 %collective-permute-start.2 = (bf16[256,3072]{1,0:T(8,128)(2,1)S(1)}, bf16[256,3072]{1,0:T(8,128)(2,1)}, u32[]{:S(2)}, u32[]{:S(2)}) collective-permute-start(bf16[256,3072]{1,0:T(8,128)(2,1)S(1)} %bitcast.12), channel_id=1, source_target_pairs={{0,1},{1,0},{2,3},{3,2},{4,5},{5,4},{6,7},{7,6},{8,9},{9,8},{10,11... | collective-permute-start | bytes 4718600 | tf_op jit(solution)/shard_map/ppermute | solution.py:316
  31.8 12.3 %collective-permute-start.9 = (bf16[32,6144]{1,0:T(8,128)(2,1)S(1)}, bf16[32,6144]{1,0:T(8,128)(2,1)S(1)}, u32[]{:S(2)}, u32[]{:S(2)}) collective-permute-start(bf16[32,6144]{1,0:T(8,128)(2,1)S(1)} %pad_maximum_fusion), channel_id=1, source_target_pairs={{0,64},{64,0},{1,65},{65,1},{2,66},{66,2},{3,67},{67,3},{4,68},{68... | collective-permute-start | bytes 1179656 | tf_op jit(solution)/shard_map/ppermute | solution.py:319
  45.4 24.2 %all-to-all-start.1 = ((bf16[8,32,3072]{2,1,0:T(8,128)(2,1)}), bf16[8,32,3072]{2,1,0:T(8,128)(2,1)S(1)}, u32[]{:S(2)}, u32[]{:S(2)}) async-start(bf16[8,32,3072]{2,1,0:T(8,128)(2,1)} %broadcast_in_dim.29), calls=%async_computation.1 | async-start | bytes 3145728 | tf_op jit(solution)/shard_map/all_to_all | solution.py:325
  49.0 26.5 %collective-permute-start.3 = (f32[128,1152]{1,0:T(8,128)}, f32[128,1152]{1,0:T(8,128)}, u32[]{:S(2)}, u32[]{:S(2)}) collective-permute-start(f32[128,1152]{1,0:T(8,128)} %get-tuple-element.35), channel_id=1, source_target_pairs={{0,16},{16,32},{32,48},{48,0},{1,17},{17,33},{33,49},{49,1},{2,18}... | collective-permute-start | bytes 1769480 | tf_op jit(solution)/shard_map/ppermute | solution.py:322
  50.3 28.0 %collective-permute-start.4 = (f32[128,1152]{1,0:T(8,128)}, f32[128,1152]{1,0:T(8,128)}, u32[]{:S(2)}, u32[]{:S(2)}) collective-permute-start(f32[128,1152]{1,0:T(8,128)} %get-tuple-element.36), channel_id=1, source_target_pairs={{0,32},{16,48},{32,0},{48,16},{1,33},{17,49},{33,1},{49,17},{2,34}... | collective-permute-start | bytes 1769480 | tf_op jit(solution)/shard_map/ppermute | solution.py:322
  52.7 25.5 %collective-permute-start.5 = (f32[128,1152]{1,0:T(8,128)}, f32[128,1152]{1,0:T(8,128)}, u32[]{:S(2)}, u32[]{:S(2)}) collective-permute-start(f32[128,1152]{1,0:T(8,128)} %get-tuple-element.37), channel_id=1, source_target_pairs={{0,48},{16,0},{32,16},{48,32},{1,49},{17,1},{33,17},{49,33},{2,50}... | collective-permute-start | bytes 1769480 | tf_op jit(solution)/shard_map/ppermute | solution.py:322
  69.7 2.2 %copy-start.1 = (bf16[8,32,3072]{2,1,0:T(8,128)(2,1)}, bf16[8,32,3072]{2,1,0:T(8,128)(2,1)S(1)}, u32[]{:S(2)}) copy-start(bf16[8,32,3072]{2,1,0:T(8,128)(2,1)S(1)} %all-to-all-done.1) | copy-start | bytes 4718596
  71.8 46.0 %all-to-all-start.2 = ((bf16[8,32,6144]{2,1,0:T(8,128)(2,1)}), bf16[8,32,6144]{2,1,0:T(8,128)(2,1)S(1)}, u32[]{:S(2)}, u32[]{:S(2)}) async-start(bf16[8,32,6144]{2,1,0:T(8,128)(2,1)} %broadcast_in_dim.30), calls=%async_computation.2 | async-start | bytes 6291456 | tf_op jit(solution)/shard_map/all_to_all | solution.py:325
  80.0 22.1 %copy-start.11 = (bf16[128,1152]{1,0:T(8,128)(2,1)}, bf16[128,1152]{1,0:T(8,128)(2,1)S(1)}, u32[]{:S(2)}) copy-start(bf16[128,1152]{1,0:T(8,128)(2,1)S(1)} %add_convert_fusion.rest_0_) | copy-start | bytes 884740
  80.0 11.6 %collective-permute-start.10 = (bf16[256,3072]{1,0:T(8,128)(2,1)}, bf16[256,3072]{1,0:T(8,128)(2,1)S(1)}, u32[]{:S(2)}, u32[]{:S(2)}) collective-permute-start(bf16[256,3072]{1,0:T(8,128)(2,1)} %bitcast.9), channel_id=1, source_target_pairs={{0,1},{1,0},{2,3},{3,2},{4,5},{5,4},{6,7},{7,6},{8,9},{9,8},{10,11... | collective-permute-start | bytes 4718600 | tf_op jit(solution)/shard_map/ppermute | solution.py:316
  81.8 9.8 %collective-permute-start.8 = (bf16[128,1152]{1,0:T(8,128)(2,1)S(1)}, bf16[128,1152]{1,0:T(8,128)(2,1)S(1)}, u32[]{:S(2)}, u32[]{:S(2)}) collective-permute-start(bf16[128,1152]{1,0:T(8,128)(2,1)S(1)} %add_convert_fusion.rest_0_), channel_id=1, source_target_pairs={{0,16},{16,32},{32,48},{48,0},{1,17},{17,33},{33,49},{49,1},{2,18}... | collective-permute-start | bytes 884744 | tf_op jit(solution)/shard_map/ppermute | solution.py:322
  82.9 8.7 %collective-permute-start.6 = (bf16[128,1152]{1,0:T(8,128)(2,1)S(1)}, bf16[128,1152]{1,0:T(8,128)(2,1)S(1)}, u32[]{:S(2)}, u32[]{:S(2)}) collective-permute-start(bf16[128,1152]{1,0:T(8,128)(2,1)S(1)} %add_convert_fusion.rest_0_), channel_id=1, source_target_pairs={{0,48},{16,0},{32,16},{48,32},{1,49},{17,1},{33,17},{49,33},{2,50}... | collective-permute-start | bytes 884744 | tf_op jit(solution)/shard_map/ppermute | solution.py:322
  91.6 5.8 %copy-start.13 = (bf16[128,1152]{1,0:T(8,128)(2,1)}, bf16[128,1152]{1,0:T(8,128)(2,1)S(1)}, u32[]{:S(2)}) copy-start(bf16[128,1152]{1,0:T(8,128)(2,1)S(1)} %collective-permute-done.8.rest_3_) | copy-start | bytes 884740
  91.6 5.8 %copy-start.14 = (bf16[128,1152]{1,0:T(8,128)(2,1)}, bf16[128,1152]{1,0:T(8,128)(2,1)S(1)}, u32[]{:S(2)}) copy-start(bf16[128,1152]{1,0:T(8,128)(2,1)S(1)} %collective-permute-done.6.rest_1_) | copy-start | bytes 884740
  91.6 1.2 copy-start.4
  97.4 7.1 %collective-permute-start.11 = (f32[128,384]{1,0:T(8,128)}, f32[128,384]{1,0:T(8,128)}, u32[]{:S(2)}, u32[]{:S(2)}) collective-permute-start(f32[128,384]{1,0:T(8,128)} %get-tuple-element.43), channel_id=1, source_target_pairs={{0,16},{16,32},{32,48},{48,0},{1,17},{17,33},{33,49},{49,1},{2,18}... | collective-permute-start | bytes 589832 | tf_op jit(solution)/shard_map/ppermute | solution.py:322
  98.0 11.3 %collective-permute-start.12 = (f32[128,384]{1,0:T(8,128)}, f32[128,384]{1,0:T(8,128)}, u32[]{:S(2)}, u32[]{:S(2)}) collective-permute-start(f32[128,384]{1,0:T(8,128)} %get-tuple-element.44), channel_id=1, source_target_pairs={{0,32},{16,48},{32,0},{48,16},{1,33},{17,49},{33,1},{49,17},{2,34}... | collective-permute-start | bytes 589832 | tf_op jit(solution)/shard_map/ppermute | solution.py:322
  101.0 9.4 %collective-permute-start.13 = (f32[128,384]{1,0:T(8,128)}, f32[128,384]{1,0:T(8,128)}, u32[]{:S(2)}, u32[]{:S(2)}) collective-permute-start(f32[128,384]{1,0:T(8,128)} %get-tuple-element.45), channel_id=1, source_target_pairs={{0,48},{16,0},{32,16},{48,32},{1,49},{17,1},{33,17},{49,33},{2,50}... | collective-permute-start | bytes 589832 | tf_op jit(solution)/shard_map/ppermute | solution.py:322
  102.0 15.8 %collective-permute-start.7 = (bf16[128,1152]{1,0:T(8,128)(2,1)S(1)}, bf16[128,1152]{1,0:T(8,128)(2,1)}, u32[]{:S(2)}, u32[]{:S(2)}) collective-permute-start(bf16[128,1152]{1,0:T(8,128)(2,1)S(1)} %add_convert_fusion.rest_0_), channel_id=1, source_target_pairs={{0,32},{16,48},{32,0},{48,16},{1,33},{17,49},{33,1},{49,17},{2,34}... | collective-permute-start | bytes 884744 | tf_op jit(solution)/shard_map/ppermute | solution.py:322
  111.6 10.0 %copy-start.12 = (bf16[128,384]{1,0:T(8,128)(2,1)}, bf16[128,384]{1,0:T(8,128)(2,1)S(1)}, u32[]{:S(2)}) copy-start(bf16[128,384]{1,0:T(8,128)(2,1)S(1)} %add_convert_fusion.1.rest_4_) | copy-start | bytes 294916
  111.6 6.4 %collective-permute-start.16 = (bf16[128,384]{1,0:T(8,128)(2,1)S(1)}, bf16[128,384]{1,0:T(8,128)(2,1)}, u32[]{:S(2)}, u32[]{:S(2)}) collective-permute-start(bf16[128,384]{1,0:T(8,128)(2,1)S(1)} %add_convert_fusion.1.rest_4_), channel_id=1, source_target_pairs={{0,16},{16,32},{32,48},{48,0},{1,17},{17,33},{33,49},{49,1},{2,18}... | collective-permute-start | bytes 294920 | tf_op jit(solution)/shard_map/ppermute | solution.py:322
  114.8 6.0 %collective-permute-start.15 = (bf16[128,384]{1,0:T(8,128)(2,1)S(1)}, bf16[128,384]{1,0:T(8,128)(2,1)}, u32[]{:S(2)}, u32[]{:S(2)}) collective-permute-start(bf16[128,384]{1,0:T(8,128)(2,1)S(1)} %add_convert_fusion.1.rest_4_), channel_id=1, source_target_pairs={{0,32},{16,48},{32,0},{48,16},{1,33},{17,49},{33,1},{49,17},{2,34}... | collective-permute-start | bytes 294920 | tf_op jit(solution)/shard_map/ppermute | solution.py:322
  116.8 4.8 %collective-permute-start.14 = (bf16[128,384]{1,0:T(8,128)(2,1)S(1)}, bf16[128,384]{1,0:T(8,128)(2,1)}, u32[]{:S(2)}, u32[]{:S(2)}) collective-permute-start(bf16[128,384]{1,0:T(8,128)(2,1)S(1)} %add_convert_fusion.1.rest_4_), channel_id=1, source_target_pairs={{0,48},{16,0},{32,16},{48,32},{1,49},{17,1},{33,17},{49,33},{2,50}... | collective-permute-start | bytes 294920 | tf_op jit(solution)/shard_map/ppermute | solution.py:322
  117.9 31.7 %copy-start = (bf16[8,32,6144]{2,1,0:T(8,128)(2,1)}, bf16[8,32,6144]{2,1,0:T(8,128)(2,1)S(1)}, u32[]{:S(2)}) copy-start(bf16[8,32,6144]{2,1,0:T(8,128)(2,1)S(1)} %all-to-all-done.2) | copy-start | bytes 9437188
  129.2 4.2 %collective-permute-start.17 = (bf16[4,256,384]{2,1,0:T(8,128)(2,1)}, bf16[4,256,384]{2,1,0:T(8,128)(2,1)S(1)}, u32[]{:S(2)}, u32[]{:S(2)}) collective-permute-start(bf16[4,256,384]{2,1,0:T(8,128)(2,1)} %get-tuple-element.49), channel_id=1, source_target_pairs={{0,1},{1,0},{2,3},{3,2},{4,5},{5,4},{6,7},{7,6},{8,9},{9,8},{10,11... | collective-permute-start | bytes 2359304 | tf_op jit(solution)/shard_map/ppermute | solution.py:316
  130.8 18.8 %collective-permute-start.18 = (bf16[4,128,384]{2,1,0:T(8,128)(2,1)}, bf16[4,128,384]{2,1,0:T(8,128)(2,1)S(1)}, u32[]{:S(2)}, u32[]{:S(2)}) collective-permute-start(bf16[4,128,384]{2,1,0:T(8,128)(2,1)} %get-tuple-element.52), channel_id=1, source_target_pairs={{0,64},{64,0},{1,65},{65,1},{2,66},{66,2},{3,67},{67,3},{4,68},{68... | collective-permute-start | bytes 1179656 | tf_op jit(solution)/shard_map/ppermute | solution.py:319
  133.4 0.9 copy-start.2
  149.6 8.2 %copy-start.7 = (bf16[4,128,384]{2,1,0:T(8,128)(2,1)}, bf16[4,128,384]{2,1,0:T(8,128)(2,1)S(1)}, u32[]{:S(2)}) copy-start(bf16[4,128,384]{2,1,0:T(8,128)(2,1)S(1)} %collective-permute-done.18.rest_0_) | copy-start | bytes 1179652
  149.6 25.5 %collective-permute-start.19 = (bf16[256,6144]{1,0:T(8,128)(2,1)S(1)}, bf16[256,6144]{1,0:T(8,128)(2,1)}, u32[]{:S(2)}, u32[]{:S(2)}) collective-permute-start(bf16[256,6144]{1,0:T(8,128)(2,1)S(1)} %bitcast.6), channel_id=1, source_target_pairs={{0,1},{1,0},{2,3},{3,2},{4,5},{5,4},{6,7},{7,6},{8,9},{9,8},{10,11... | collective-permute-start | bytes 9437192 | tf_op jit(solution)/shard_map/ppermute | solution.py:316
  150.0 42.5 %all-to-all-start.3 = ((bf16[8,2,32,3072]{3,2,1,0:T(8,128)(2,1)}), bf16[8,2,32,3072]{3,2,1,0:T(8,128)(2,1)}, u32[]{:S(2)}, u32[]{:S(2)}) async-start(bf16[8,2,32,3072]{3,2,1,0:T(8,128)(2,1)} %shard_map.80), calls=%async_computation.3 | async-start | bytes 6291456 | tf_op jit(solution)/shard_map/all_to_all | solution.py:325
  154.6 16.5 %collective-permute-start.22 = (bf16[4,128,384]{2,1,0:T(8,128)(2,1)S(1)}, bf16[4,128,384]{2,1,0:T(8,128)(2,1)S(1)}, u32[]{:S(2)}, u32[]{:S(2)}) collective-permute-start(bf16[4,128,384]{2,1,0:T(8,128)(2,1)S(1)} %collective-permute-done.18.rest_0_), channel_id=1, source_target_pairs={{0,16},{16,32},{32,48},{48,0},{1,17},{17,33},{33,49},{49,1},{2,18}... | collective-permute-start | bytes 1179656 | tf_op jit(solution)/shard_map/ppermute | solution.py:322
  155.1 20.0 %collective-permute-start.21 = (bf16[4,128,384]{2,1,0:T(8,128)(2,1)S(1)}, bf16[4,128,384]{2,1,0:T(8,128)(2,1)S(1)}, u32[]{:S(2)}, u32[]{:S(2)}) collective-permute-start(bf16[4,128,384]{2,1,0:T(8,128)(2,1)S(1)} %collective-permute-done.18.rest_0_), channel_id=1, source_target_pairs={{0,32},{16,48},{32,0},{48,16},{1,33},{17,49},{33,1},{49,17},{2,34}... | collective-permute-start | bytes 1179656 | tf_op jit(solution)/shard_map/ppermute | solution.py:322
  157.8 17.4 %collective-permute-start.20 = (bf16[4,128,384]{2,1,0:T(8,128)(2,1)S(1)}, bf16[4,128,384]{2,1,0:T(8,128)(2,1)S(1)}, u32[]{:S(2)}, u32[]{:S(2)}) collective-permute-start(bf16[4,128,384]{2,1,0:T(8,128)(2,1)S(1)} %collective-permute-done.18.rest_0_), channel_id=1, source_target_pairs={{0,48},{16,0},{32,16},{48,32},{1,49},{17,1},{33,17},{49,33},{2,50}... | collective-permute-start | bytes 1179656 | tf_op jit(solution)/shard_map/ppermute | solution.py:322
  171.0 4.1 %copy-start.8 = (bf16[4,128,384]{2,1,0:T(8,128)(2,1)}, bf16[4,128,384]{2,1,0:T(8,128)(2,1)S(1)}, u32[]{:S(2)}) copy-start(bf16[4,128,384]{2,1,0:T(8,128)(2,1)S(1)} %collective-permute-done.22.rest_3_) | copy-start | bytes 1179652
  175.1 0.7 copy-start.9
  175.1 0.9 copy-start.10
where the time goes:
time: 197 us; the launch traced here: 196 us
  Pallas kernels  69.7 us (35%)
  starting transfers between devices  46.1 us (23%)
  waiting for transfers between devices  37.4 us (19%)
  blocking collectives  26.5 us (13%)
  local copies, waits for them, and re-layouts  8.38 us (4%)
  other arithmetic  6.94 us (4%)
    pallas_call x8, Pallas kernels, run(): pl.pallas_call(kernel, grid=grid, in_specs=in_specs, out_specs=out_specs,...  69.7 us
    all_to_all x1, blocking collectives, among_chips(): return lax.all_to_all(x, 'colxdept', 0, 0, axis_index_groups=same_core)  26.5 us
    ppermute x15, starting transfers between devices, along_row(): lax.ppermute(x, 'row', [(i, (i + step) % n_row) for i in range(n_row)])  21.7 us
    ppermute x15, waiting for transfers between devices, along_row(): lax.ppermute(x, 'row', [(i, (i + step) % n_row) for i in range(n_row)])  20.3 us
    all_to_all x3, waiting for transfers between devices, among_chips(): return lax.all_to_all(x, 'colxdept', 0, 0, axis_index_groups=same_core)  16.5 us
    all_to_all x3, starting transfers between devices, among_chips(): return lax.all_to_all(x, 'colxdept', 0, 0, axis_index_groups=same_core)  11.7 us
    ppermute x6, starting transfers between devices, swap_cores(): return lax.ppermute(x, 'colxdept', [(i, i ^ 1) for i in range(n_col)])  7.34 us
    ppermute x2, starting transfers between devices, swap_dp(): return lax.ppermute(x, 'dp', [(i, (i + 1) % n_dp) for i in range(n_dp)])  5.33 us
  transfers between devices with their start and end apart: 26, of which 13 were waited for; matrix products, arithmetic and copies ran while one was open for 4% of the time, Pallas kernels for 32%

commit v1 on v0

--- a/solution.py
+++ b/solution.py
@@ -19,7 +19,7 @@
     return lax.dot_general(a, b, dims, preferred_element_type=F32)
 
 
-def call(kernel, grid, in_specs, out_specs, out_shape, flops, scratch=(), aliases=None):
+def call(kernel, grid, in_specs, out_specs, out_shape, flops, scratch=()):
     def run(*args):
         many = out_shape if isinstance(out_shape, list) else [out_shape]
         moved = sum(a.size * a.dtype.itemsize for a in [*args, *many])
@@ -30,7 +30,6 @@
             out_specs=out_specs,
             out_shape=out_shape,
             scratch_shapes=list(scratch),
-            input_output_aliases=aliases or {},
             compiler_params=pltpu.CompilerParams(vmem_limit_bytes=ROOM),
             cost_estimate=pl.CostEstimate(flops=flops, bytes_accessed=moved, transcendentals=0),
         )(*args)
@@ -183,50 +182,32 @@
     )(row, rows, cols, *pieces, *back_pieces)
 
 
-def mix(chips, done, done_sib, w, w_sib):
-    width, depth = w.shape
+def partials(chips, done, done_sib, w_out, w_out_sib, w_qkv, w_qkv_sib):
+    n, depth, width = w_qkv.shape
     half = done_sib.shape[1]
-    step = min(1024, depth)
-
-    def kernel(d, ds, w, ws, out):
-        out[...] = (dot(d[...], w[...]) + dot(ds[...], ws[...])).astype(BF16).reshape(out.shape)
-
-    d_spec = spec((None, half, width), lambda m: (0, 0, 0))
-    w_spec = spec((width, step), lambda m: (0, m))
+    step = min(512, depth)
+
+    def side(x, first):
+        return jnp.concatenate([x[a] for a in range(first, n + first)], axis=1)
+
+    def kernel(d, ds, wo, wos, wq, wqs, out):
+        mixed = dot(d[0], wo[...]) + dot(ds[0], wos[...])
+        out[:, 0] = mixed.astype(BF16).reshape(out.shape[0], *out.shape[2:])
+        grads = jnp.concatenate([side(d, 1), side(ds, 1)], axis=1)
+        weights = jnp.concatenate([side(wq, 0), side(wqs, 0)], axis=1)
+        out[:, 1] = dot(grads, weights, NT).astype(BF16).reshape(out.shape[0], *out.shape[2:])
+
+    d_spec = spec((n + 1, half, width), lambda m: (0, 0, 0))
+    o_spec = spec((width, step), lambda m: (0, m))
+    q_spec = spec((n, step, width), lambda m: (0, m, 0))
     return call(
         kernel,
         (depth // step,),
-        [d_spec, d_spec, w_spec, w_spec],
-        spec((chips, None, half // chips, step), lambda m: (0, 0, 0, m)),
+        [d_spec, d_spec, o_spec, o_spec, q_spec, q_spec],
+        spec((chips, 2, half // chips, step), lambda m: (0, 0, 0, m)),
         jax.ShapeDtypeStruct((chips, 2, half // chips, depth), BF16),
-        4 * half * depth * width,
-    )(done, done_sib, w, w_sib)
-
-
-def back_tokens(first, done, done_sib, w, w_sib):
-    n, depth, width = w.shape
-    chips, half = first.shape[0], done_sib.shape[1]
-    step = min(512, depth)
-
-    def side(x, start):
-        return [x[a] for a in range(start, n + start)]
-
-    def kernel(_, d, ds, w, ws, out):
-        grads = jnp.concatenate(side(d, 1) + side(ds, 1), axis=1)
-        weights = jnp.concatenate(side(w, 0) + side(ws, 0), axis=1)
-        out[...] = dot(grads, weights, NT).astype(BF16).reshape(out.shape)
-
-    d_spec = spec((n + 1, half, width), lambda m: (0, 0, 0))
-    w_spec = spec((n, step, width), lambda m: (0, m, 0))
-    return call(
-        kernel,
-        (depth // step,),
-        [pl.BlockSpec(memory_space=pl.ANY), d_spec, d_spec, w_spec, w_spec],
-        spec((chips, None, half // chips, step), lambda m: (0, 1, 0, m)),
-        jax.ShapeDtypeStruct(first.shape, BF16),
-        4 * half * n * depth * width,
-        aliases={0: 0},
-    )(first, done, done_sib, w, w_sib)
+        4 * half * (n + 1) * depth * width,
+    )(done, done_sib, w_out, w_out_sib, w_qkv, w_qkv_sib)
 
 
 def weight_own(tok_mine, tok_sib, cot_mine, cot_sib, done):
@@ -361,8 +342,7 @@
     done, second, quarter = attention(at, rows, cols, pieces, back_pieces)
     quarter = swap_dp(quarter)
     done_sib = swap_cores(second)
-    first = mix(chips, done, done_sib, w_out, w_out_sib)
-    both = back_tokens(first, done, done_sib, w_qkv, w_qkv_sib)
+    both = partials(chips, done, done_sib, w_out, w_out_sib, w_qkv, w_qkv_sib)
     both, quarter, other_mine = lax.optimization_barrier((both, quarter, other_mine))
     done2 = gather_row(quarter)
     other_sib = swap_cores(other_mine)
@@ -370,8 +350,8 @@
     own_qkv, own_out = weight_own(tok_mine, tok_sib, cot_mine, cot_sib, after(done, both))
     grad_qkv, grad_out = weight_both(at, own_qkv, own_out, other_mine, other_sib, done2)
     shares = after(shares, grad_out, grad_qkv)
-    results = jnp.sum(shares.astype(F32), axis=0).astype(BF16)
-    return (results[:1], results[1:], grad_qkv, grad_out)
+    mixed, grad_tokens = [jnp.sum(shares[:, a].astype(F32), axis=0).astype(BF16) for a in range(2)]
+    return (mixed[None], grad_tokens[None], grad_qkv, grad_out)
 
 
 def solution(mesh):

time: 197 us -> 194 us (0.985)
  Pallas kernels: 69.7 us -> 66.3 us
    pallas_call x8 -> x7, Pallas kernels: 69.7 us -> 66.3 us  [run(): pl.pallas_call(kernel, grid=grid, in_specs=in_specs, out_specs=out_specs,...]
  transfers between devices with their start and end apart: 26 -> 26, of which waited for: 13 -> 13; matrix products, arithmetic and copies ran while one was open for 4% -> 4% of each run, Pallas kernels for 32% -> 30%
where the time goes in v1:
time: 194 us; the launch traced here: 193 us
  Pallas kernels  66.3 us (34%)
  starting transfers between devices  46.1 us (24%)
  waiting for transfers between devices  37.5 us (19%)
  blocking collectives  26.5 us (14%)
  other arithmetic  7.89 us (4%)
  local copies, waits for them, and re-layouts  7.67 us (4%)
    pallas_call x7, Pallas kernels, run(): pl.pallas_call(kernel, grid=grid, in_specs=in_specs, out_specs=out_specs,...  66.3 us
    all_to_all x1, blocking collectives, among_chips(): return lax.all_to_all(x, 'colxdept', 0, 0, axis_index_groups=same_core)  26.5 us
    ppermute x15, starting transfers between devices, along_row(): lax.ppermute(x, 'row', [(i, (i + step) % n_row) for i in range(n_row)])  21.7 us
    ppermute x15, waiting for transfers between devices, along_row(): lax.ppermute(x, 'row', [(i, (i + step) % n_row) for i in range(n_row)])  20.5 us
    all_to_all x3, waiting for transfers between devices, among_chips(): return lax.all_to_all(x, 'colxdept', 0, 0, axis_index_groups=same_core)  16.5 us
    all_to_all x3, starting transfers between devices, among_chips(): return lax.all_to_all(x, 'colxdept', 0, 0, axis_index_groups=same_core)  11.7 us
    ppermute x6, starting transfers between devices, swap_cores(): return lax.ppermute(x, 'colxdept', [(i, i ^ 1) for i in range(n_col)])  7.31 us
    ppermute x2, starting transfers between devices, swap_dp(): return lax.ppermute(x, 'dp', [(i, (i + 1) % n_dp) for i in range(n_dp)])  5.33 us
  transfers between devices with their start and end apart: 26, of which 13 were waited for; matrix products, arithmetic and copies ran while one was open for 4% of the time, Pallas kernels for 30%

profile of v1, /device:TPU:1, one launch (start us, length us, event | category | flops | bytes accessed | tf_op | source)
XLA Modules:
  0.0 192.8 jit_solution(15660506056770418220)
XLA Ops:
  0.6 1.5 collective-permute-start.1
  2.2 1.2 broadcast_in_dim.33
  3.4 26.5 %all_to_all.20 = bf16[8,32,3072]{2,1,0:T(8,128)(2,1)S(1)} all-to-all(bf16[8,32,3072]{2,1,0:T(8,128)(2,1)S(1)} %broadcast_in_dim.33), channel_id=1, replica_groups={{0,2,4,6,8,10,12,14},{1,3,5,7,9,11,13,15},{16,18,20,22,24,26,28,30},{17..., dimensions={0} | all-to-all | bytes 3145728 | tf_op jit(solution)/shard_map/all_to_all | solution.py:306
  29.9 1.9 %collective-permute-start.2 = (bf16[256,3072]{1,0:T(8,128)(2,1)S(1)}, bf16[256,3072]{1,0:T(8,128)(2,1)}, u32[]{:S(2)}, u32[]{:S(2)}) collective-permute-start(bf16[256,3072]{1,0:T(8,128)(2,1)S(1)} %bitcast.14), channel_id=1, source_target_pairs={{0,1},{1,0},{2,3},{3,2},{4,5},{5,4},{6,7},{7,6},{8,9},{9,8},{10,11... | collective-permute-start | bytes 4718600 | tf_op jit(solution)/shard_map/ppermute | solution.py:297
  31.9 2.7 %collective-permute-start.9 = (bf16[32,6144]{1,0:T(8,128)(2,1)S(1)}, bf16[32,6144]{1,0:T(8,128)(2,1)S(1)}, u32[]{:S(2)}, u32[]{:S(2)}) collective-permute-start(bf16[32,6144]{1,0:T(8,128)(2,1)S(1)} %pad_maximum_fusion), channel_id=1, source_target_pairs={{0,64},{64,0},{1,65},{65,1},{2,66},{66,2},{3,67},{67,3},{4,68},{68... | collective-permute-start | bytes 1179656 | tf_op jit(solution)/shard_map/ppermute | solution.py:300
  35.0 9.1 %shard_map.75 = (f32[128,1152]{1,0:T(8,128)}, f32[128,1152]{1,0:T(8,128)}, f32[128,1152]{1,0:T(8,128)}, f32[128,1152]{1,0:T(8,128)}) custom-call(s32[1]{0:T(128)} %bitcast.row, bf16[256,3072]{1,0:T(8,128)(2,1)} %bitcast.15, bf16[256,3072]{1,0:T(8,128)(2,1)} %collective-permute-done.2.sib.t1, bf16[3,3072,384]{2,1,0:T(8,128)(2,1)} %wq.1), custom_call_target="tpu_custom_call" | custom-call | flops 3623878656 | bytes 12582916 | tf_op jit(solution)/shard_map/pallas_call | solution.py:26
  44.2 1.3 broadcast_in_dim.35
  45.5 3.6 %all-to-all-start.1 = ((bf16[8,32,3072]{2,1,0:T(8,128)(2,1)}), bf16[8,32,3072]{2,1,0:T(8,128)(2,1)S(1)}, u32[]{:S(2)}, u32[]{:S(2)}) async-start(bf16[8,32,3072]{2,1,0:T(8,128)(2,1)} %broadcast_in_dim.35), calls=%async_computation.1 | async-start | bytes 3145728 | tf_op jit(solution)/shard_map/all_to_all | solution.py:306
  49.1 1.3 collective-permute-start.3
  50.4 2.5 %collective-permute-start.4 = (f32[128,1152]{1,0:T(8,128)}, f32[128,1152]{1,0:T(8,128)}, u32[]{:S(2)}, u32[]{:S(2)}) collective-permute-start(f32[128,1152]{1,0:T(8,128)} %get-tuple-element.36), channel_id=1, source_target_pairs={{0,32},{16,48},{32,0},{48,16},{1,33},{17,49},{33,1},{49,17},{2,34}... | collective-permute-start | bytes 1769480 | tf_op jit(solution)/shard_map/ppermute | solution.py:303
  52.8 1.2 collective-permute-start.5
  54.0 15.8 %all-to-all-done.1 = bf16[8,32,3072]{2,1,0:T(8,128)(2,1)S(1)} async-done(((bf16[8,32,3072]{2,1,0:T(8,128)(2,1)}), bf16[8,32,3072]{2,1,0:T(8,128)(2,1)S(1)}, u32[]{:S(2)}, u32[]{:S(2)}) %all-to-all-start.1) | async-done | bytes 1572896 | tf_op jit(solution)/shard_map/all_to_all | solution.py:306
  69.7 2.2 %broadcast_in_dim.36 = bf16[8,32,6144]{2,1,0:T(8,128)(2,1)} broadcast(bf16[32,6144]{1,0:T(8,128)(2,1)S(1)} %collective-permute-done.9), dimensions={1,2} | broadcast | bytes 3538944 | tf_op jit(solution)/shard_map/broadcast_in_dim | solution.py:309
  71.9 3.7 %all-to-all-start.2 = ((bf16[8,32,6144]{2,1,0:T(8,128)(2,1)}), bf16[8,32,6144]{2,1,0:T(8,128)(2,1)S(1)}, u32[]{:S(2)}, u32[]{:S(2)}) async-start(bf16[8,32,6144]{2,1,0:T(8,128)(2,1)} %broadcast_in_dim.36), calls=%async_computation.2 | async-start | bytes 6291456 | tf_op jit(solution)/shard_map/all_to_all | solution.py:306
  75.6 2.7 %collective-permute-done.4 = f32[128,1152]{1,0:T(8,128)} collective-permute-done((f32[128,1152]{1,0:T(8,128)}, f32[128,1152]{1,0:T(8,128)}, u32[]{:S(2)}, u32[]{:S(2)}) %collective-permute-start.4) | collective-permute-done | bytes 589856 | tf_op jit(solution)/shard_map/ppermute | solution.py:303
  78.3 1.7 add_convert_fusion.rest_0_
  80.0 1.8 collective-permute-start.10
  81.8 1.1 collective-permute-start.8
  82.9 1.6 collective-permute-start.6
  84.5 4.3 %shard_map.76.mine = f32[256,384]{1,0:T(8,128)} custom-call(bf16[256,3072]{1,0:T(8,128)(2,1)} %bitcast.11, bf16[384,3072]{1,0:T(8,128)(2,1)} %wo.1), custom_call_target="tpu_custom_call" | custom-call | flops 603979776 | bytes 4325376 | tf_op jit(solution)/shard_map/pallas_call | solution.py:26
  88.8 2.8 %collective-permute-done.8.rest_3_ = bf16[128,1152]{1,0:T(8,128)(2,1)S(1)} collective-permute-done((bf16[128,1152]{1,0:T(8,128)(2,1)S(1)}, bf16[128,1152]{1,0:T(8,128)(2,1)S(1)}, u32[]{:S(2)}, u32[]{:S(2)}) %collective-permute-start.8) | collective-permute-done | bytes 294944 | tf_op jit(solution)/shard_map/ppermute | solution.py:303
  91.7 1.2 copy-done.4
  92.8 4.6 %shard_map.77 = (f32[128,384]{1,0:T(8,128)}, f32[128,384]{1,0:T(8,128)}, f32[128,384]{1,0:T(8,128)}, f32[128,384]{1,0:T(8,128)}) custom-call(s32[1]{0:T(128)} %bitcast.row, f32[256,384]{1,0:T(8,128)} %shard_map.76.mine, bf16[256,3072]{1,0:T(8,128)(2,1)} %copy-done.4, bf16[384,3072]{1,0:T(8,128)(2,1)} %wo.1), custom_call_target="tpu_custom_call" | custom-call | flops 603979776 | bytes 5111812 | tf_op jit(solution)/shard_map/pallas_call | solution.py:26
  98.0 3.0 %collective-permute-start.12 = (f32[128,384]{1,0:T(8,128)}, f32[128,384]{1,0:T(8,128)}, u32[]{:S(2)}, u32[]{:S(2)}) collective-permute-start(f32[128,384]{1,0:T(8,128)} %get-tuple-element.44), channel_id=1, source_target_pairs={{0,32},{16,48},{32,0},{48,16},{1,33},{17,49},{33,1},{49,17},{2,34}... | collective-permute-start | bytes 589832 | tf_op jit(solution)/shard_map/ppermute | solution.py:303
  101.2 0.9 fusion.4.rows
  102.1 1.4 collective-permute-start.7
  103.4 1.1 collective-permute-done.11
  104.6 4.7 %collective-permute-done.12 = f32[128,384]{1,0:T(8,128)} collective-permute-done((f32[128,384]{1,0:T(8,128)}, f32[128,384]{1,0:T(8,128)}, u32[]{:S(2)}, u32[]{:S(2)}) %collective-permute-start.12) | collective-permute-done | bytes 196640 | tf_op jit(solution)/shard_map/ppermute | solution.py:303
  109.3 1.1 collective-permute-done.13
  110.4 1.3 add_convert_fusion.1.rest_4_
  111.7 3.1 %collective-permute-start.16 = (bf16[128,384]{1,0:T(8,128)(2,1)S(1)}, bf16[128,384]{1,0:T(8,128)(2,1)}, u32[]{:S(2)}, u32[]{:S(2)}) collective-permute-start(bf16[128,384]{1,0:T(8,128)(2,1)S(1)} %add_convert_fusion.1.rest_4_), channel_id=1, source_target_pairs={{0,16},{16,32},{32,48},{48,0},{1,17},{17,33},{33,49},{49,1},{2,18}... | collective-permute-start | bytes 294920 | tf_op jit(solution)/shard_map/ppermute | solution.py:303
  114.8 2.0 %collective-permute-start.15 = (bf16[128,384]{1,0:T(8,128)(2,1)S(1)}, bf16[128,384]{1,0:T(8,128)(2,1)}, u32[]{:S(2)}, u32[]{:S(2)}) collective-permute-start(bf16[128,384]{1,0:T(8,128)(2,1)S(1)} %add_convert_fusion.1.rest_4_), channel_id=1, source_target_pairs={{0,32},{16,48},{32,0},{48,16},{1,33},{17,49},{33,1},{49,17},{2,34}... | collective-permute-start | bytes 294920 | tf_op jit(solution)/shard_map/ppermute | solution.py:303
  117.3 0.6 fusion.18.cols
  118.1 2.8 %collective-permute-done.15.rest_6_ = bf16[128,384]{1,0:T(8,128)(2,1)} collective-permute-done((bf16[128,384]{1,0:T(8,128)(2,1)S(1)}, bf16[128,384]{1,0:T(8,128)(2,1)}, u32[]{:S(2)}, u32[]{:S(2)}) %collective-permute-start.15) | collective-permute-done | bytes 98336 | tf_op jit(solution)/shard_map/ppermute | solution.py:303
  120.8 0.8 collective-permute-done.14.rest_5_
  121.7 7.6 %shard_map.78 = (bf16[4,512,384]{2,1,0:T(8,128)(2,1)}, bf16[4,256,384]{2,1,0:T(8,128)(2,1)}, bf16[4,128,384]{2,1,0:T(8,128)(2,1)}) custom-call(s32[1]{0:T(128)} %bitcast.row, s32[512,1]{1,0:T(8,128)} %fusion.4.rows, s32[1,512]{1,0:T(1,128)} %fusion.18.cols, bf16[128,1152]{1,0:T(8,128)(2,1)} %copy-done.12, bf16[128,1152]{1,0:T(8,128)(2,1)} %copy-done.15, ...), custom_call_target="tpu_custom_call" | custom-call | flops 1409286144 | bytes 4329476 | tf_op jit(solution)/shard_map/pallas_call | solution.py:26
  129.3 1.5 collective-permute-start.17
  130.8 2.6 %collective-permute-start.18 = (bf16[4,128,384]{2,1,0:T(8,128)(2,1)}, bf16[4,128,384]{2,1,0:T(8,128)(2,1)S(1)}, u32[]{:S(2)}, u32[]{:S(2)}) collective-permute-start(bf16[4,128,384]{2,1,0:T(8,128)(2,1)} %get-tuple-element.52), channel_id=1, source_target_pairs={{0,64},{64,0},{1,65},{65,1},{2,66},{66,2},{3,67},{67,3},{4,68},{68... | collective-permute-start | bytes 1179656 | tf_op jit(solution)/shard_map/ppermute | solution.py:300
  133.5 0.9 copy-done.5
  134.4 12.0 %shard_map.79 = bf16[8,2,32,3072]{3,2,1,0:T(8,128)(2,1)} custom-call(bf16[4,512,384]{2,1,0:T(8,128)(2,1)} %get-tuple-element.54.d, bf16[4,256,384]{2,1,0:T(8,128)(2,1)} %copy-done.5, bf16[384,3072]{1,0:T(8,128)(2,1)} %wo.1, bf16[384,3072]{1,0:T(8,128)(2,1)} %collective-permute-done.wos, bf16[3,3072,384]{2,1,0:T(8,128)(2,1)} %wq.1, ...), custom_call_target="tpu_custom_call" | custom-call | flops 4831838208 | bytes 24379392 | tf_op jit(solution)/shard_map/pallas_call | solution.py:26
  146.8 4.5 %all-to-all-start.3 = ((bf16[8,2,32,3072]{3,2,1,0:T(8,128)(2,1)}), bf16[8,2,32,3072]{3,2,1,0:T(8,128)(2,1)}, u32[]{:S(2)}, u32[]{:S(2)}) async-start(bf16[8,2,32,3072]{3,2,1,0:T(8,128)(2,1)} %shard_map.79), calls=%async_computation.3 | async-start | bytes 6291456 | tf_op jit(solution)/shard_map/all_to_all | solution.py:306
  151.9 2.6 %collective-permute-start.21 = (bf16[4,128,384]{2,1,0:T(8,128)(2,1)S(1)}, bf16[4,128,384]{2,1,0:T(8,128)(2,1)S(1)}, u32[]{:S(2)}, u32[]{:S(2)}) collective-permute-start(bf16[4,128,384]{2,1,0:T(8,128)(2,1)S(1)} %collective-permute-done.18.rest_0_), channel_id=1, source_target_pairs={{0,32},{16,48},{32,0},{48,16},{1,33},{17,49},{33,1},{49,17},{2,34}... | collective-permute-start | bytes 1179656 | tf_op jit(solution)/shard_map/ppermute | solution.py:303
  154.7 13.0 %shard_map.80 = (f32[3,3072,384]{2,1,0:T(8,128)}, f32[384,3072]{1,0:T(8,128)}) custom-call(bf16[256,3072]{1,0:T(8,128)(2,1)} %bitcast.16, bf16[256,3072]{1,0:T(8,128)(2,1)} %collective-permute-done.2.sib.t1, bf16[256,3072]{1,0:T(8,128)(2,1)} %bitcast.12, bf16[256,3072]{1,0:T(8,128)(2,1)} %copy-done.4, bf16[4,512,384]{2,1,0:T(8,128)(2,1)} %get-tuple-element.54.d), custom_call_target="tpu_custom_call" | custom-call | flops 4831838208 | bytes 26738688 | tf_op jit(solution)/shard_map/pallas_call | solution.py:26
  167.8 4.1 %collective-permute-done.21.rest_2_ = bf16[4,128,384]{2,1,0:T(8,128)(2,1)S(1)} collective-permute-done((bf16[4,128,384]{2,1,0:T(8,128)(2,1)S(1)}, bf16[4,128,384]{2,1,0:T(8,128)(2,1)S(1)}, u32[]{:S(2)}, u32[]{:S(2)}) %collective-permute-start.21) | collective-permute-done | bytes 393248 | tf_op jit(solution)/shard_map/ppermute | solution.py:303
  171.9 0.7 copy-done.10
  172.8 15.8 %shard_map.81 = (bf16[3,3072,384]{2,1,0:T(8,128)(2,1)}, bf16[384,3072]{1,0:T(8,128)(2,1)}) custom-call(s32[1]{0:T(128)} %bitcast.row, f32[3,3072,384]{2,1,0:T(8,128)} %get-tuple-element.55.q, f32[384,3072]{1,0:T(8,128)} %get-tuple-element.56.o, bf16[256,6144]{1,0:T(8,128)(2,1)} %bitcast.9, bf16[256,6144]{1,0:T(8,128)(2,1)} %collective-permute-done.19.t1.c1, ...), custom_call_target="tpu_custom_call" | custom-call | flops 4831838208 | bytes 42467332 | tf_op jit(solution)/shard_map/pallas_call | solution.py:26
  188.6 0.8 all-to-all-done.3
  189.4 3.4 %slice_reduce_fusion = (bf16[32,3072]{1,0:T(8,128)(2,1)}, bf16[32,3072]{1,0:T(8,128)(2,1)}) fusion(bf16[8,2,32,3072]{3,2,1,0:T(8,128)(2,1)} %all-to-all-done.3), kind=kLoop, calls=%fused_computation | loop fusion | flops 1376256 | bytes 3538944 | tf_op jit(solution)/shard_map/reduce_sum | solution.py:353
  (53 shorter events, 3.5 us)
Async XLA Ops:
  0.6 29.2 %collective-permute-start.1 = (bf16[3,3072,384]{2,1,0:T(8,128)(2,1)}, bf16[3,3072,384]{2,1,0:T(8,128)(2,1)}, u32[]{:S(2)}, u32[]{:S(2)}) collective-permute-start(bf16[3,3072,384]{2,1,0:T(8,128)(2,1)} %wq.1), channel_id=1, source_target_pairs={{0,1},{1,0},{2,3},{3,2},{4,5},{5,4},{6,7},{7,6},{8,9},{9,8},{10,11... | collective-permute-start | bytes 21233672 | tf_op jit(solution)/shard_map/ppermute | solution.py:297
  2.1 27.7 %collective-permute-start = (bf16[384,3072]{1,0:T(8,128)(2,1)}, bf16[384,3072]{1,0:T(8,128)(2,1)}, u32[]{:S(2)}, u32[]{:S(2)}) collective-permute-start(bf16[384,3072]{1,0:T(8,128)(2,1)} %wo.1), channel_id=1, source_target_pairs={{0,1},{1,0},{2,3},{3,2},{4,5},{5,4},{6,7},{7,6},{8,9},{9,8},{10,11... | collective-permute-start | bytes 7077896 | tf_op jit(solution)/shard_map/ppermute | solution.py:297
  2.2 29.6 %copy-start.6 = (bf16[1,32,3072]{2,1,0:T(8,128)(2,1)S(1)}, bf16[1,32,3072]{2,1,0:T(8,128)(2,1)}, u32[]{:S(2)}) copy-start(bf16[1,32,3072]{2,1,0:T(8,128)(2,1)} %param.4) | copy-start | bytes 589828
  2.2 29.6 %copy-start.7 = (bf16[1,32,3072]{2,1,0:T(8,128)(2,1)S(1)}, bf16[1,32,3072]{2,1,0:T(8,128)(2,1)}, u32[]{:S(2)}) copy-start(bf16[1,32,3072]{2,1,0:T(8,128)(2,1)} %param.7) | copy-start | bytes 589828
  29.9 5.1 %copy-start.3 = (bf16[8,32,3072]{2,1,0:T(8,128)(2,1)}, bf16[8,32,3072]{2,1,0:T(8,128)(2,1)S(1)}, u32[]{:S(2)}) copy-start(bf16[8,32,3072]{2,1,0:T(8,128)(2,1)S(1)} %all_to_all.20) | copy-start | bytes 4718596
  29.9 5.1 %collective-permute-start.2 = (bf16[256,3072]{1,0:T(8,128)(2,1)S(1)}, bf16[256,3072]{1,0:T(8,128)(2,1)}, u32[]{:S(2)}, u32[]{:S(2)}) collective-permute-start(bf16[256,3072]{1,0:T(8,128)(2,1)S(1)} %bitcast.14), channel_id=1, source_target_pairs={{0,1},{1,0},{2,3},{3,2},{4,5},{5,4},{6,7},{7,6},{8,9},{9,8},{10,11... | collective-permute-start | bytes 4718600 | tf_op jit(solution)/shard_map/ppermute | solution.py:297
  31.9 12.3 %collective-permute-start.9 = (bf16[32,6144]{1,0:T(8,128)(2,1)S(1)}, bf16[32,6144]{1,0:T(8,128)(2,1)S(1)}, u32[]{:S(2)}, u32[]{:S(2)}) collective-permute-start(bf16[32,6144]{1,0:T(8,128)(2,1)S(1)} %pad_maximum_fusion), channel_id=1, source_target_pairs={{0,64},{64,0},{1,65},{65,1},{2,66},{66,2},{3,67},{67,3},{4,68},{68... | collective-permute-start | bytes 1179656 | tf_op jit(solution)/shard_map/ppermute | solution.py:300
  45.5 24.2 %all-to-all-start.1 = ((bf16[8,32,3072]{2,1,0:T(8,128)(2,1)}), bf16[8,32,3072]{2,1,0:T(8,128)(2,1)S(1)}, u32[]{:S(2)}, u32[]{:S(2)}) async-start(bf16[8,32,3072]{2,1,0:T(8,128)(2,1)} %broadcast_in_dim.35), calls=%async_computation.1 | async-start | bytes 3145728 | tf_op jit(solution)/shard_map/all_to_all | solution.py:306
  49.1 26.5 %collective-permute-start.3 = (f32[128,1152]{1,0:T(8,128)}, f32[128,1152]{1,0:T(8,128)}, u32[]{:S(2)}, u32[]{:S(2)}) collective-permute-start(f32[128,1152]{1,0:T(8,128)} %get-tuple-element.35), channel_id=1, source_target_pairs={{0,16},{16,32},{32,48},{48,0},{1,17},{17,33},{33,49},{49,1},{2,18}... | collective-permute-start | bytes 1769480 | tf_op jit(solution)/shard_map/ppermute | solution.py:303
  50.4 28.0 %collective-permute-start.4 = (f32[128,1152]{1,0:T(8,128)}, f32[128,1152]{1,0:T(8,128)}, u32[]{:S(2)}, u32[]{:S(2)}) collective-permute-start(f32[128,1152]{1,0:T(8,128)} %get-tuple-element.36), channel_id=1, source_target_pairs={{0,32},{16,48},{32,0},{48,16},{1,33},{17,49},{33,1},{49,17},{2,34}... | collective-permute-start | bytes 1769480 | tf_op jit(solution)/shard_map/ppermute | solution.py:303
  52.8 25.5 %collective-permute-start.5 = (f32[128,1152]{1,0:T(8,128)}, f32[128,1152]{1,0:T(8,128)}, u32[]{:S(2)}, u32[]{:S(2)}) collective-permute-start(f32[128,1152]{1,0:T(8,128)} %get-tuple-element.37), channel_id=1, source_target_pairs={{0,48},{16,0},{32,16},{48,32},{1,49},{17,1},{33,17},{49,33},{2,50}... | collective-permute-start | bytes 1769480 | tf_op jit(solution)/shard_map/ppermute | solution.py:303
  69.7 2.2 %copy-start.1 = (bf16[8,32,3072]{2,1,0:T(8,128)(2,1)}, bf16[8,32,3072]{2,1,0:T(8,128)(2,1)S(1)}, u32[]{:S(2)}) copy-start(bf16[8,32,3072]{2,1,0:T(8,128)(2,1)S(1)} %all-to-all-done.1) | copy-start | bytes 4718596
  71.9 46.0 %all-to-all-start.2 = ((bf16[8,32,6144]{2,1,0:T(8,128)(2,1)}), bf16[8,32,6144]{2,1,0:T(8,128)(2,1)S(1)}, u32[]{:S(2)}, u32[]{:S(2)}) async-start(bf16[8,32,6144]{2,1,0:T(8,128)(2,1)} %broadcast_in_dim.36), calls=%async_computation.2 | async-start | bytes 6291456 | tf_op jit(solution)/shard_map/all_to_all | solution.py:306
  75.6 4.5 %copy-start.2 = (bf16[8,32,3072]{2,1,0:T(8,128)(2,1)S(1)}, bf16[8,32,3072]{2,1,0:T(8,128)(2,1)}, u32[]{:S(2)}) copy-start(bf16[8,32,3072]{2,1,0:T(8,128)(2,1)} %copy-done.1) | copy-start | bytes 4718596
  80.0 22.0 %copy-start.12 = (bf16[128,1152]{1,0:T(8,128)(2,1)}, bf16[128,1152]{1,0:T(8,128)(2,1)S(1)}, u32[]{:S(2)}) copy-start(bf16[128,1152]{1,0:T(8,128)(2,1)S(1)} %add_convert_fusion.rest_0_) | copy-start | bytes 884740
  80.0 11.6 %collective-permute-start.10 = (bf16[256,3072]{1,0:T(8,128)(2,1)S(1)}, bf16[256,3072]{1,0:T(8,128)(2,1)S(1)}, u32[]{:S(2)}, u32[]{:S(2)}) collective-permute-start(bf16[256,3072]{1,0:T(8,128)(2,1)S(1)} %bitcast.13), channel_id=1, source_target_pairs={{0,1},{1,0},{2,3},{3,2},{4,5},{5,4},{6,7},{7,6},{8,9},{9,8},{10,11... | collective-permute-start | bytes 4718600 | tf_op jit(solution)/shard_map/ppermute | solution.py:297
  81.8 9.8 %collective-permute-start.8 = (bf16[128,1152]{1,0:T(8,128)(2,1)S(1)}, bf16[128,1152]{1,0:T(8,128)(2,1)S(1)}, u32[]{:S(2)}, u32[]{:S(2)}) collective-permute-start(bf16[128,1152]{1,0:T(8,128)(2,1)S(1)} %add_convert_fusion.rest_0_), channel_id=1, source_target_pairs={{0,16},{16,32},{32,48},{48,0},{1,17},{17,33},{33,49},{49,1},{2,18}... | collective-permute-start | bytes 884744 | tf_op jit(solution)/shard_map/ppermute | solution.py:303
  82.9 8.7 %collective-permute-start.6 = (bf16[128,1152]{1,0:T(8,128)(2,1)S(1)}, bf16[128,1152]{1,0:T(8,128)(2,1)S(1)}, u32[]{:S(2)}, u32[]{:S(2)}) collective-permute-start(bf16[128,1152]{1,0:T(8,128)(2,1)S(1)} %add_convert_fusion.rest_0_), channel_id=1, source_target_pairs={{0,48},{16,0},{32,16},{48,32},{1,49},{17,1},{33,17},{49,33},{2,50}... | collective-permute-start | bytes 884744 | tf_op jit(solution)/shard_map/ppermute | solution.py:303
  91.6 5.8 %copy-start.14 = (bf16[128,1152]{1,0:T(8,128)(2,1)}, bf16[128,1152]{1,0:T(8,128)(2,1)S(1)}, u32[]{:S(2)}) copy-start(bf16[128,1152]{1,0:T(8,128)(2,1)S(1)} %collective-permute-done.8.rest_3_) | copy-start | bytes 884740
  91.6 5.8 %copy-start.15 = (bf16[128,1152]{1,0:T(8,128)(2,1)}, bf16[128,1152]{1,0:T(8,128)(2,1)S(1)}, u32[]{:S(2)}) copy-start(bf16[128,1152]{1,0:T(8,128)(2,1)S(1)} %collective-permute-done.6.rest_1_) | copy-start | bytes 884740
  91.6 1.2 copy-start.4
  97.4 7.2 %collective-permute-start.11 = (f32[128,384]{1,0:T(8,128)}, f32[128,384]{1,0:T(8,128)}, u32[]{:S(2)}, u32[]{:S(2)}) collective-permute-start(f32[128,384]{1,0:T(8,128)} %get-tuple-element.43), channel_id=1, source_target_pairs={{0,16},{16,32},{32,48},{48,0},{1,17},{17,33},{33,49},{49,1},{2,18}... | collective-permute-start | bytes 589832 | tf_op jit(solution)/shard_map/ppermute | solution.py:303
  98.0 11.3 %collective-permute-start.12 = (f32[128,384]{1,0:T(8,128)}, f32[128,384]{1,0:T(8,128)}, u32[]{:S(2)}, u32[]{:S(2)}) collective-permute-start(f32[128,384]{1,0:T(8,128)} %get-tuple-element.44), channel_id=1, source_target_pairs={{0,32},{16,48},{32,0},{48,16},{1,33},{17,49},{33,1},{49,17},{2,34}... | collective-permute-start | bytes 589832 | tf_op jit(solution)/shard_map/ppermute | solution.py:303
  101.0 9.4 %collective-permute-start.13 = (f32[128,384]{1,0:T(8,128)}, f32[128,384]{1,0:T(8,128)}, u32[]{:S(2)}, u32[]{:S(2)}) collective-permute-start(f32[128,384]{1,0:T(8,128)} %get-tuple-element.45), channel_id=1, source_target_pairs={{0,48},{16,0},{32,16},{48,32},{1,49},{17,1},{33,17},{49,33},{2,50}... | collective-permute-start | bytes 589832 | tf_op jit(solution)/shard_map/ppermute | solution.py:303
  102.1 15.8 %collective-permute-start.7 = (bf16[128,1152]{1,0:T(8,128)(2,1)S(1)}, bf16[128,1152]{1,0:T(8,128)(2,1)}, u32[]{:S(2)}, u32[]{:S(2)}) collective-permute-start(bf16[128,1152]{1,0:T(8,128)(2,1)S(1)} %add_convert_fusion.rest_0_), channel_id=1, source_target_pairs={{0,32},{16,48},{32,0},{48,16},{1,33},{17,49},{33,1},{49,17},{2,34}... | collective-permute-start | bytes 884744 | tf_op jit(solution)/shard_map/ppermute | solution.py:303
  111.7 10.0 %copy-start.13 = (bf16[128,384]{1,0:T(8,128)(2,1)}, bf16[128,384]{1,0:T(8,128)(2,1)S(1)}, u32[]{:S(2)}) copy-start(bf16[128,384]{1,0:T(8,128)(2,1)S(1)} %add_convert_fusion.1.rest_4_) | copy-start | bytes 294916
  111.7 6.4 %collective-permute-start.16 = (bf16[128,384]{1,0:T(8,128)(2,1)S(1)}, bf16[128,384]{1,0:T(8,128)(2,1)}, u32[]{:S(2)}, u32[]{:S(2)}) collective-permute-start(bf16[128,384]{1,0:T(8,128)(2,1)S(1)} %add_convert_fusion.1.rest_4_), channel_id=1, source_target_pairs={{0,16},{16,32},{32,48},{48,0},{1,17},{17,33},{33,49},{49,1},{2,18}... | collective-permute-start | bytes 294920 | tf_op jit(solution)/shard_map/ppermute | solution.py:303
  114.8 6.0 %collective-permute-start.15 = (bf16[128,384]{1,0:T(8,128)(2,1)S(1)}, bf16[128,384]{1,0:T(8,128)(2,1)}, u32[]{:S(2)}, u32[]{:S(2)}) collective-permute-start(bf16[128,384]{1,0:T(8,128)(2,1)S(1)} %add_convert_fusion.1.rest_4_), channel_id=1, source_target_pairs={{0,32},{16,48},{32,0},{48,16},{1,33},{17,49},{33,1},{49,17},{2,34}... | collective-permute-start | bytes 294920 | tf_op jit(solution)/shard_map/ppermute | solution.py:303
  116.9 4.8 %collective-permute-start.14 = (bf16[128,384]{1,0:T(8,128)(2,1)S(1)}, bf16[128,384]{1,0:T(8,128)(2,1)}, u32[]{:S(2)}, u32[]{:S(2)}) collective-permute-start(bf16[128,384]{1,0:T(8,128)(2,1)S(1)} %add_convert_fusion.1.rest_4_), channel_id=1, source_target_pairs={{0,48},{16,0},{32,16},{48,32},{1,49},{17,1},{33,17},{49,33},{2,50}... | collective-permute-start | bytes 294920 | tf_op jit(solution)/shard_map/ppermute | solution.py:303
  117.9 28.5 %copy-start = (bf16[8,32,6144]{2,1,0:T(8,128)(2,1)}, bf16[8,32,6144]{2,1,0:T(8,128)(2,1)S(1)}, u32[]{:S(2)}) copy-start(bf16[8,32,6144]{2,1,0:T(8,128)(2,1)S(1)} %all-to-all-done.2) | copy-start | bytes 9437188
  129.3 4.2 %collective-permute-start.17 = (bf16[4,256,384]{2,1,0:T(8,128)(2,1)}, bf16[4,256,384]{2,1,0:T(8,128)(2,1)S(1)}, u32[]{:S(2)}, u32[]{:S(2)}) collective-permute-start(bf16[4,256,384]{2,1,0:T(8,128)(2,1)} %get-tuple-element.49), channel_id=1, source_target_pairs={{0,1},{1,0},{2,3},{3,2},{4,5},{5,4},{6,7},{7,6},{8,9},{9,8},{10,11... | collective-permute-start | bytes 2359304 | tf_op jit(solution)/shard_map/ppermute | solution.py:297
  130.8 15.6 %collective-permute-start.18 = (bf16[4,128,384]{2,1,0:T(8,128)(2,1)}, bf16[4,128,384]{2,1,0:T(8,128)(2,1)S(1)}, u32[]{:S(2)}, u32[]{:S(2)}) collective-permute-start(bf16[4,128,384]{2,1,0:T(8,128)(2,1)} %get-tuple-element.52), channel_id=1, source_target_pairs={{0,64},{64,0},{1,65},{65,1},{2,66},{66,2},{3,67},{67,3},{4,68},{68... | collective-permute-start | bytes 1179656 | tf_op jit(solution)/shard_map/ppermute | solution.py:300
  133.5 0.9 copy-start.5
  146.4 8.1 %copy-start.8 = (bf16[4,128,384]{2,1,0:T(8,128)(2,1)}, bf16[4,128,384]{2,1,0:T(8,128)(2,1)S(1)}, u32[]{:S(2)}) copy-start(bf16[4,128,384]{2,1,0:T(8,128)(2,1)S(1)} %collective-permute-done.18.rest_0_) | copy-start | bytes 1179652
  146.4 25.5 %collective-permute-start.19 = (bf16[256,6144]{1,0:T(8,128)(2,1)S(1)}, bf16[256,6144]{1,0:T(8,128)(2,1)}, u32[]{:S(2)}, u32[]{:S(2)}) collective-permute-start(bf16[256,6144]{1,0:T(8,128)(2,1)S(1)} %bitcast.8), channel_id=1, source_target_pairs={{0,1},{1,0},{2,3},{3,2},{4,5},{5,4},{6,7},{7,6},{8,9},{9,8},{10,11... | collective-permute-start | bytes 9437192 | tf_op jit(solution)/shard_map/ppermute | solution.py:297
  146.8 42.5 %all-to-all-start.3 = ((bf16[8,2,32,3072]{3,2,1,0:T(8,128)(2,1)}), bf16[8,2,32,3072]{3,2,1,0:T(8,128)(2,1)}, u32[]{:S(2)}, u32[]{:S(2)}) async-start(bf16[8,2,32,3072]{3,2,1,0:T(8,128)(2,1)} %shard_map.79), calls=%async_computation.3 | async-start | bytes 6291456 | tf_op jit(solution)/shard_map/all_to_all | solution.py:306
  151.3 16.4 %collective-permute-start.22 = (bf16[4,128,384]{2,1,0:T(8,128)(2,1)S(1)}, bf16[4,128,384]{2,1,0:T(8,128)(2,1)S(1)}, u32[]{:S(2)}, u32[]{:S(2)}) collective-permute-start(bf16[4,128,384]{2,1,0:T(8,128)(2,1)S(1)} %collective-permute-done.18.rest_0_), channel_id=1, source_target_pairs={{0,16},{16,32},{32,48},{48,0},{1,17},{17,33},{33,49},{49,1},{2,18}... | collective-permute-start | bytes 1179656 | tf_op jit(solution)/shard_map/ppermute | solution.py:303
  151.9 20.0 %collective-permute-start.21 = (bf16[4,128,384]{2,1,0:T(8,128)(2,1)S(1)}, bf16[4,128,384]{2,1,0:T(8,128)(2,1)S(1)}, u32[]{:S(2)}, u32[]{:S(2)}) collective-permute-start(bf16[4,128,384]{2,1,0:T(8,128)(2,1)S(1)} %collective-permute-done.18.rest_0_), channel_id=1, source_target_pairs={{0,32},{16,48},{32,0},{48,16},{1,33},{17,49},{33,1},{49,17},{2,34}... | collective-permute-start | bytes 1179656 | tf_op jit(solution)/shard_map/ppermute | solution.py:303
  154.5 17.4 %collective-permute-start.20 = (bf16[4,128,384]{2,1,0:T(8,128)(2,1)S(1)}, bf16[4,128,384]{2,1,0:T(8,128)(2,1)S(1)}, u32[]{:S(2)}, u32[]{:S(2)}) collective-permute-start(bf16[4,128,384]{2,1,0:T(8,128)(2,1)S(1)} %collective-permute-done.18.rest_0_), channel_id=1, source_target_pairs={{0,48},{16,0},{32,16},{48,32},{1,49},{17,1},{33,17},{49,33},{2,50}... | collective-permute-start | bytes 1179656 | tf_op jit(solution)/shard_map/ppermute | solution.py:303
  167.8 4.2 %copy-start.9 = (bf16[4,128,384]{2,1,0:T(8,128)(2,1)}, bf16[4,128,384]{2,1,0:T(8,128)(2,1)S(1)}, u32[]{:S(2)}) copy-start(bf16[4,128,384]{2,1,0:T(8,128)(2,1)S(1)} %collective-permute-done.22.rest_3_) | copy-start | bytes 1179652
  171.9 0.7 copy-start.10
  171.9 0.9 copy-start.11
